TPU v7x, 128 devices: a whole 4x4x4 slice. The times are simulated.
128 devices in a mesh: seq: 32 (over x, y, core), exp: 4 (over z).
Axes of the slice: x: 4, y: 4, z: 4, core: 2. Of those that a mesh axis runs over, the one named last changes fastest.
Arguments:
- query_states: bfloat16 [4096, 4096], P('seq', 'exp'), may hold values from -5 to 5
- key_states: bfloat16 [4096, 4096], P('seq', 'exp'), may hold values from -5 to 5
- value_states: bfloat16 [4096, 4096], P('seq', 'exp'), may hold values from -6 to 6
- selected: int32 [32, 3], replicated, may hold values from 0 to 30, as said below
- residual: bfloat16 [4096, 7168], P('seq', 'exp'), may hold values from -15 to 15
- out_weight: bfloat16 [32, 128, 7168], P('exp', 'seq'), may hold values from -0.25 to 0.25
- norm_gain: bfloat16 [7168], P('exp'), may hold values from 0.5 to 1.5
- w_gate: bfloat16 [128, 7168, 512], P(('seq', 'exp')), may hold values from -0.0625 to 0.0625
- w_up: bfloat16 [128, 7168, 512], P(('seq', 'exp')), may hold values from -0.0625 to 0.0625
- w_down: bfloat16 [128, 512, 7168], P(('seq', 'exp')), may hold values from -0.1875 to 0.1875
- routes: int32 [4096, 8], P('seq'), may hold values from 0 to 63, all different within a row; in each aligned block of 128 rows (0 to 127, 128 to 255, ...) at most 20 rows name the same one
- route_weights: bfloat16 [4096, 8], P('seq'), may hold values from 0.099609375 to 0.59765625
Outputs:
- layer_out: bfloat16 [4096, 7168], P('seq', 'exp')
Inputs may be any that keep to these rules, and one draw needn't show every extreme that they name: `selected`: for a block b of at least 3, row b holds 3 different earlier blocks, among them b - 1; for b under 3, it holds every earlier block once and b itself in the remaining entries. `routes`: each row names 8 different experts; in each aligned block of 128 rows (the tokens of one index of seq) no expert is named by more than 20 rows.
All inputs are finite; a program needn't handle non-finite values.
Results may differ from a plain program's by a relative error of at most 0.02.
Values may be sent and summed in bfloat16 or wider, within the bound.
No kernel may reach another device: no remote copies, remote signals or barrier semaphores. Data moves between devices by JAX's collectives and lax.ppermute only.
A program may use at most 128 MiB of HBM per device.

v0:
```python
import math

import jax
import jax.numpy as jnp
from jax import lax
from jax.experimental import pallas as pl
from jax.experimental.pallas import tpu as pltpu
from jax.sharding import PartitionSpec as P

EPSILON = 1e-06
NEGATIVE = -1e30
CAP = 20
DIRECT = 12
SWAPPED = CAP - DIRECT
EARLY = 240
STEP = 1792
OUT_STEP = 896
MIB = 2**20
BF16 = jnp.bfloat16
F32 = jnp.float32


def dot(a, b):
    return jnp.dot(a, b, preferred_element_type=F32)


def dot_rows(a, b):
    return lax.dot_general(a, b, (((0,), (0,)), ((), ())), preferred_element_type=F32)


def half_swap(block):
    return lax.ppermute(block, "exp", [(i, i ^ 1) for i in range(4)])


def group_swap(block):
    return lax.ppermute(block, "exp", [(i, 3 - i) for i in range(4)])


def spread(block):
    return lax.all_to_all(block, "seq", split_axis=0, concat_axis=0, tiled=True)


def fetch_blocks(key_states, value_states, selected):
    count = lax.axis_size("seq")
    rows, width = key_states.shape
    piece = 2 * rows // count
    stacked = jnp.concatenate([key_states, value_states], axis=0)
    pieces = spread(stacked).reshape(count, piece, width)
    previous = lax.ppermute(stacked, "seq", [(i, i + 1) for i in range(count - 1)])
    before = jnp.arange(count, dtype=jnp.int32)[:, None] - 1
    place = jnp.argmax(selected == before, axis=1)
    first = jnp.where(place == 0, selected[:, 1], selected[:, 0])
    second = jnp.where(place == 2, selected[:, 1], selected[:, 2])
    others = jnp.stack([first, second], axis=1)
    wanted = jnp.take(pieces, others.reshape(-1), axis=0).reshape(-1, width)
    fetched = spread(wanted)
    return fetched, previous, others


def attend(query_states, key_states, value_states, selected, heads):
    position = lax.axis_index("seq")
    rows, width = query_states.shape
    head_dim = width // heads
    fetched, previous, others = fetch_blocks(key_states, value_states, selected)
    keys = jnp.concatenate([fetched[: 2 * rows], previous[:rows], key_states], axis=0)
    values = jnp.concatenate([fetched[2 * rows :], previous[rows:], value_states], axis=0)
    keys = keys.reshape(-1, heads, head_dim)
    values = values.reshape(-1, heads, head_dim)
    queries = query_states.reshape(rows, heads, head_dim)
    scores = jnp.einsum("qhd,khd->hqk", queries, keys, preferred_element_type=F32) * (
        1.0 / math.sqrt(head_dim)
    )
    mine = lax.dynamic_slice_in_dim(others, position, 1, 0)[0] < position
    turn = jnp.arange(2 * rows, dtype=jnp.int32) // (2 * rows // lax.axis_size("seq")) % 2
    far = jnp.where(turn == 0, mine[0], mine[1])
    far = jnp.concatenate([far, jnp.broadcast_to(position > 0, (rows,))])
    places = jnp.arange(rows, dtype=jnp.int32)
    causal = places[None, :] <= places[:, None]
    visible = jnp.concatenate(
        [jnp.broadcast_to(far[None, :], (rows, far.shape[0])), causal], axis=1
    )
    scores = jnp.where(visible[None], scores, NEGATIVE)
    peak = jnp.max(scores, axis=2, keepdims=True)
    weights = jnp.exp(scores - peak)
    total = jnp.sum(weights, axis=2, keepdims=True)
    soft_weights = (weights / total).astype(BF16)
    attended = jnp.einsum("hqk,khd->qhd", soft_weights, values, preferred_element_type=F32)
    return attended.astype(BF16).reshape(rows, width)


def regroup(attended, heads, pieces):
    width = attended.shape[1]
    head_dim = width // heads
    piece = head_dim // pieces
    old = jnp.arange(width, dtype=jnp.int32)
    new_of_old = (old % head_dim) // piece * (heads * piece) + old // head_dim * piece + old % piece
    move = (new_of_old[:, None] == jnp.arange(width, dtype=jnp.int32)[None, :]).astype(BF16)
    return dot(attended, move).astype(BF16)


def project_sum(attended, full_out, order, theirs_order, width, behind):
    def product(index):
        columns = lax.dynamic_slice_in_dim(full_out, index * width, width, 1)
        return dot(attended, columns).astype(BF16)

    given = [half_swap(product(theirs_order[n])) for n in range(2)]
    kept = [product(order[n]) for n in range(2)]
    given[0], behind = lax.optimization_barrier((given[0], behind))
    pairs = [(a.astype(F32) + b.astype(F32)).astype(BF16) for a, b in zip(kept, given)]
    total = [pair.astype(F32) + group_swap(pair).astype(F32) for pair in pairs]
    return jnp.concatenate(total, axis=1), behind


def lane_sums(block):
    total = block[:, :128]
    for low in range(128, block.shape[1], 128):
        total = total + block[:, low : low + 128]
    return total


def gated(gate, up):
    return (gate / (1.0 + jnp.exp(-gate)) * up).astype(BF16)


def call(kernel, vmem, order, steps, in_specs, out_specs, out_shape, scratch, *args):
    return pl.pallas_call(
        kernel,
        grid_spec=pltpu.PrefetchScalarGridSpec(
            num_scalar_prefetch=1,
            grid=(steps,),
            in_specs=in_specs,
            out_specs=out_specs,
            scratch_shapes=scratch,
        ),
        out_shape=out_shape,
        compiler_params=pltpu.CompilerParams(
            dimension_semantics=("arbitrary",), vmem_limit_bytes=vmem * MIB
        ),
        cost_estimate=pl.CostEstimate(flops=1000, bytes_accessed=1000, transcendentals=0),
    )(order, *args)


def whole(shape):
    return pl.BlockSpec(shape, lambda k, order: (0,) * len(shape))


def weight_rows(per_slice, units):
    return pl.BlockSpec(
        (1, STEP, units), lambda k, order: (0, order[k // per_slice] * per_slice + k % per_slice, 0)
    )


def half_units(block, gain_half, order, w_gate, w_up, before=None):
    rows, width = block.shape
    units = w_gate.shape[2]
    steps = width // STEP

    def kernel(order_ref, x_ref, gain_ref, wg_ref, wu_ref, *refs):
        k = pl.program_id(0)
        if before is None:
            gate_ref, up_ref, square_ref = refs
        else:
            gate_in, up_in, square_in, act_ref, gate_ref, up_ref, square_ref = refs

        @pl.when(k == 0)
        def _():
            for ref, start in zip(
                (gate_ref, up_ref, square_ref), (None,) * 3 if before is None else refs[:3]
            ):
                ref[...] = jnp.zeros_like(ref) if start is None else start[...]

        x = x_ref[...]
        gate_ref[...] += dot(x, wg_ref[0])
        up_ref[...] += dot(x, wu_ref[0])
        plain = x.astype(F32) * (1.0 / gain_ref[...].astype(F32))
        square_ref[...] += lane_sums(plain * plain)
        if before is not None:

            @pl.when(k == steps - 1)
            def _():
                total = jnp.sum(square_ref[...], axis=1, keepdims=True)
                scale = lax.rsqrt(total / (2 * width) + EPSILON)
                act_ref[...] = gated(gate_ref[...] * scale, up_ref[...] * scale)

    per_slice = steps // 2
    in_specs = [
        pl.BlockSpec((rows, STEP), lambda k, order: (0, k)),
        pl.BlockSpec((1, STEP), lambda k, order: (0, k)),
        weight_rows(per_slice, units),
        weight_rows(per_slice, units),
    ]
    sums = [(rows, units), (rows, units), (rows, 128)]
    args = [block, gain_half, w_gate, w_up]
    if before is None:
        return call(
            kernel,
            20,
            order,
            steps,
            in_specs,
            [whole(shape) for shape in sums],
            [jax.ShapeDtypeStruct(shape, F32) for shape in sums],
            [],
            *args,
        )
    return call(
        kernel,
        20,
        order,
        steps,
        in_specs + [whole(shape) for shape in sums],
        whole((rows, units)),
        jax.ShapeDtypeStruct((rows, units), BF16),
        [pltpu.VMEM(shape, F32) for shape in sums],
        *args,
        *before,
    )


def unpacker(slots, groups):
    row = jnp.arange(groups * slots, dtype=jnp.int32)
    low = row // slots * 2 * slots + row % slots
    place = jnp.concatenate([low, low + slots])
    return (place[:, None] == jnp.arange(groups * 2 * slots, dtype=jnp.int32)[None, :]).astype(BF16)


def packed_units(block, slots, groups, order, w_gate, w_up):
    packed, width = block.shape
    rows = packed // 2
    units = w_gate.shape[2]
    steps = width // STEP
    part = groups * slots
    pick = unpacker(slots, groups)
    per_slice = steps // 2

    def rows_of(k, order):
        step = k // 2
        return (0, order[k % 2 * 2 + step // per_slice] * per_slice + step % per_slice, 0)

    weights = pl.BlockSpec((1, STEP, units), rows_of)

    def kernel(order_ref, x_ref, pick_ref, wg_ref, wu_ref, act_ref, row_ref, gate_ref, up_ref):
        k = pl.program_id(0)

        @pl.when(k == 0)
        def _():
            gate_ref[...] = jnp.zeros_like(gate_ref)
            up_ref[...] = jnp.zeros_like(up_ref)

        @pl.when(k % 2 == 0)
        def _():
            for b in range(rows // part):
                both = dot(pick_ref[...], x_ref[2 * b * part : 2 * (b + 1) * part, :]).astype(BF16)
                row_ref[0, b * part : (b + 1) * part, :] = both[:part]
                row_ref[1, b * part : (b + 1) * part, :] = both[part:]

        x = row_ref[k % 2]
        gate_ref[...] += dot(x, wg_ref[0])
        up_ref[...] += dot(x, wu_ref[0])

        @pl.when(k == 2 * steps - 1)
        def _():
            act_ref[...] = gated(gate_ref[...], up_ref[...])

    return call(
        kernel,
        40,
        order,
        2 * steps,
        [
            pl.BlockSpec((packed, STEP), lambda k, order: (0, k // 2)),
            whole(pick.shape),
            weights,
            weights,
        ],
        whole((rows, units)),
        jax.ShapeDtypeStruct((rows, units), BF16),
        [pltpu.VMEM((2, rows, STEP), BF16)] + [pltpu.VMEM((rows, units), F32)] * 2,
        block,
        pick,
        w_gate,
        w_up,
    )


def packed_out(act, slots, groups, order, w_down, down_theirs):
    act_theirs = half_swap(act)
    rows, units = act.shape
    width = down_theirs[0].shape[1]
    per_slice = width // OUT_STEP
    part = groups * slots
    place = unpacker(slots, groups).T

    def kernel(order_ref, mine_ref, theirs_ref, place_ref, *refs):
        low_mine, high_mine, low_theirs, high_theirs, out_ref = refs
        low = dot(mine_ref[...], low_mine[0]) + dot(theirs_ref[...], low_theirs[...])
        high = dot(mine_ref[...], high_mine[0]) + dot(theirs_ref[...], high_theirs[...])
        low, high = low.astype(BF16), high.astype(BF16)
        for b in range(rows // part):
            here = slice(b * part, (b + 1) * part)
            both = dot(place_ref[...], jnp.concatenate([low[here], high[here]], axis=0))
            out_ref[2 * b * part : 2 * (b + 1) * part, :] = both.astype(BF16)

    def columns(number):
        return pl.BlockSpec((1, units, OUT_STEP), lambda k, order: (0, 0, order[number] * per_slice + k))

    return call(
        kernel,
        40,
        order,
        per_slice,
        [whole((rows, units)), whole((rows, units)), whole(place.shape), columns(0), columns(1)]
        + [pl.BlockSpec((units, OUT_STEP), lambda k, order: (0, k))] * 2,
        pl.BlockSpec((2 * rows, OUT_STEP), lambda k, order: (0, k)),
        jax.ShapeDtypeStruct((2 * rows, width), BF16),
        [],
        act,
        act_theirs,
        place,
        w_down,
        w_down,
        *down_theirs,
    )


def per_device(
    query_states,
    key_states,
    value_states,
    selected,
    residual,
    out_weight,
    norm_gain,
    w_gate,
    w_up,
    w_down,
    routes,
    route_weights,
):
    count = lax.axis_size("seq")
    exp = lax.axis_index("exp")
    rows, width = residual.shape
    heads = out_weight.shape[0]
    model_width = 4 * width
    group = exp // 2
    side = (exp >= 2).astype(jnp.int32)
    half = jnp.where(jnp.logical_or(exp == 0, exp == 3), 0, 1)
    other = 1 - half

    def ordered(mine, theirs):
        lower = side == 0
        return jnp.concatenate(
            [jnp.where(lower, mine, theirs), jnp.where(lower, theirs, mine)], axis=1
        )

    order = jnp.stack([half, 3 - half, other, 3 - other])
    theirs_order = jnp.stack([other, 3 - other, half, 3 - half])

    full_out = lax.all_gather(out_weight.reshape(-1, model_width), "seq", axis=0, tiled=True)
    gain = norm_gain[None, :]
    gain_mine = ordered(gain, group_swap(gain))
    gain_theirs = half_swap(gain_mine)
    residual_half = ordered(residual, group_swap(residual))

    down_given = [
        lax.dynamic_slice_in_dim(w_down[0], theirs_order[n] * width, width, 1) for n in range(2)
    ]
    down_given, gain_theirs = lax.optimization_barrier((down_given, gain_theirs))
    early = [half_swap(down_given[0]), half_swap(down_given[1][:EARLY])]

    experts = 2 * jnp.arange(count, dtype=jnp.int32) + group
    named = routes.T[:, None, :] == experts[None, :, None]
    hits = jnp.any(named, axis=0)
    token_weight = jnp.sum(jnp.where(named, route_weights.T[:, None, :].astype(F32), 0.0), axis=0)
    steps = jnp.arange(rows, dtype=jnp.int32)
    earlier = (steps[:, None] < steps[None, :]).astype(BF16)
    rank = jnp.where(hits, dot(hits.astype(BF16), earlier).astype(jnp.int32), -1)

    def slots(first, number):
        ids = first + jnp.arange(number, dtype=jnp.int32)
        return rank[:, None, :] == ids[None, :, None]

    def picker(mask):
        return mask.astype(BF16).reshape(-1, mask.shape[-1])

    def weigher(mask, high):
        empty = jnp.zeros_like(mask)
        mask = jnp.where(
            high,
            jnp.concatenate([empty, mask], axis=1),
            jnp.concatenate([mask, empty], axis=1),
        )
        return jnp.where(mask, token_weight[:, None, :], 0.0).astype(BF16).reshape(-1, rows)

    first = slots(0, SWAPPED)
    last = slots(SWAPPED, DIRECT)
    empty = jnp.zeros_like(last)
    pick_last = jnp.concatenate(
        [
            picker(jnp.concatenate([last, empty], axis=1)),
            picker(jnp.concatenate([empty, last], axis=1)),
        ],
        axis=1,
    )

    attended = attend(query_states, key_states, value_states, selected, heads)
    attended = regroup(attended, heads, count)
    attended, early, residual_half = lax.optimization_barrier((attended, early, residual_half))
    total, late = project_sum(
        attended, full_out, order, theirs_order, width, down_given[1][EARLY:]
    )
    late = half_swap(late)
    hidden = (total + residual_half.astype(F32)).astype(BF16).astype(F32)
    gained = (hidden * gain_mine.astype(F32)).astype(BF16)
    gained_other = half_swap(gained)

    received = spread(dot(picker(first), gained).astype(BF16))
    halves = [(gained, gain_mine), (gained_other, gain_theirs)]
    squares = sum(
        jnp.sum(jnp.square(block.astype(F32) / gain_half.astype(F32)), axis=1, keepdims=True)
        for block, gain_half in halves
    )
    scale = lax.rsqrt(squares / model_width + EPSILON)
    both = jnp.concatenate([(block.astype(F32) * scale).astype(BF16) for block, _ in halves], axis=0)
    rows_out = dot(pick_last, both).astype(BF16)
    rows_out, received, late = lax.optimization_barrier((rows_out, received, late))
    down_theirs = [early[0], jnp.concatenate([early[1], late], axis=0)]
    received_last = spread(rows_out)

    before = half_units(received, gain_mine, order, w_gate, w_up)
    act = half_units(half_swap(received), gain_theirs, theirs_order, w_gate, w_up, before)
    first_out = packed_out(act, SWAPPED, 128 // SWAPPED, order, w_down, down_theirs)
    first_out, received_last = lax.optimization_barrier((first_out, received_last))
    first_out = spread(first_out)
    act = packed_units(received_last, DIRECT, 96 // DIRECT, order, w_gate, w_up)
    last_out = packed_out(act, DIRECT, 96 // DIRECT, order, w_down, down_theirs)
    last_out, first_out = lax.optimization_barrier((last_out, first_out))
    last_out = spread(last_out)

    high = side == 0
    give = dot_rows(weigher(first, high), first_out)
    keep = dot_rows(weigher(first, ~high), first_out)
    keep = keep + jnp.where(high, hidden[:, :width], hidden[:, width:])
    give_last, keep_last = weigher(last, high), weigher(last, ~high)
    last_out, give, keep, give_last, keep_last = lax.optimization_barrier(
        (last_out, give, keep, give_last, keep_last)
    )
    give = group_swap((give + dot_rows(give_last, last_out)).astype(BF16))
    keep = keep + dot_rows(keep_last, last_out)
    return (keep + give.astype(F32)).astype(BF16)


def solution(mesh):
    return jax.shard_map(
        per_device,
        mesh=mesh,
        in_specs=(
            P("seq", "exp"),
            P("seq", "exp"),
            P("seq", "exp"),
            P(),
            P("seq", "exp"),
            P("exp", "seq", None),
            P("exp"),
            P(("seq", "exp"), None, None),
            P(("seq", "exp"), None, None),
            P(("seq", "exp"), None, None),
            P("seq", None),
            P("seq", None),
        ),
        out_specs=P("seq", "exp"),
        check_vma=False,
    )
```

profile of v0, /device:TPU:0, one launch (start us, length us, event | category | flops | bytes accessed | tf_op | source)
XLA Modules:
  0.0 370.2 jit_solution(2044371223431557592)
XLA Ops:
  6.5 1.9 reshape.220
  9.2 4.1 %collective-permute-start.1 = (bf16[1,1792]{1,0:T(2,128)(2,1)S(1)}, bf16[1,1792]{1,0:T(2,128)(2,1)S(1)}, u32[]{:S(2)}, u32[]{:S(2)}) collective-permute-start(bf16[1,1792]{1,0:T(2,128)(2,1)S(1)} %broadcast_in_dim.131), channel_id=1, source_target_pairs={{0,3},{1,2},{2,1},{3,0},{4,7},{5,6},{6,5},{7,4},{8,11},{9,10},{10,... | collective-permute-start | bytes 10760 | tf_op jit(solution)/shard_map/ppermute | solution.py:36
  13.3 1.7 constant_dynamic-update-slice_fusion.1
  15.0 1.7 constant_dynamic-update-slice_fusion
  16.7 2.2 collective-permute-start
  18.9 8.0 %all-to-all-start = ((bf16[32,8,1024]{2,1,0:T(8,128)(2,1)}), bf16[32,8,1024]{2,1,0:T(8,128)(2,1)S(1)}, u32[]{:S(2)}, u32[]{:S(2)}) async-start(bf16[32,8,1024]{2,1,0:T(8,128)(2,1)} %bitcast.13), calls=%async_computation | async-start | bytes 1048576 | tf_op jit(solution)/shard_map/all_to_all | solution.py:40
  30.0 3.6 dynamic-slice_bitcast_fusion
  35.9 1.6 collective-permute-done.2.gain_ref
  38.8 1.7 collective-permute-start.3
  41.7 1.6 gather_fusion
  43.3 2.4 bitcast_select_fusion.2
  45.6 6.2 %all-to-all-start.1 = ((bf16[32,16,1024]{2,1,0:T(8,128)(2,1)}), bf16[32,16,1024]{2,1,0:T(8,128)(2,1)S(1)}, u32[]{:S(2)}, u32[]{:S(2)}) async-start(bf16[32,16,1024]{2,1,0:T(8,128)(2,1)} %bitcast_select_fusion.2), calls=%async_computation.1 | async-start | bytes 2097152 | tf_op jit(solution)/shard_map/all_to_all | solution.py:40
  54.1 1.9 fusion.141
  58.0 1.8 copy.46
  59.7 19.3 %all-to-all-done.1 = bf16[32,16,1024]{2,1,0:T(8,128)(2,1)S(1)} async-done(((bf16[32,16,1024]{2,1,0:T(8,128)(2,1)}), bf16[32,16,1024]{2,1,0:T(8,128)(2,1)S(1)}, u32[]{:S(2)}, u32[]{:S(2)}) %all-to-all-start.1) | async-done | bytes 1048608 | tf_op jit(solution)/shard_map/all_to_all | solution.py:40
  80.6 3.2 fusion.144
  83.8 2.4 convolution_convert_fusion.2
  87.1 11.4 %collective-permute-done.3.refs_2_ = bf16[512,1792]{1,0:T(8,128)(2,1)S(1)} collective-permute-done((bf16[512,1792]{1,0:T(8,128)(2,1)}, bf16[512,1792]{1,0:T(8,128)(2,1)S(1)}, u32[]{:S(2)}, u32[]{:S(2)}) %collective-permute-start.3) | collective-permute-done | bytes 1835040 | tf_op jit(solution)/shard_map/ppermute | solution.py:32
  98.6 3.3 fusion.24
  102.9 2.2 slice.54
  105.1 2.7 fusion.39
  107.8 1.3 collective-permute-start.8
  109.2 6.3 %collective-permute-done.6 = bf16[128,1792]{1,0:T(8,128)(2,1)S(1)} collective-permute-done((bf16[128,1792]{1,0:T(8,128)(2,1)S(1)}, bf16[128,1792]{1,0:T(8,128)(2,1)S(1)}, u32[]{:S(2)}, u32[]{:S(2)}) %collective-permute-start.6) | collective-permute-done | bytes 458784 | tf_op jit(solution)/shard_map/ppermute | solution.py:32
  115.5 2.7 fusion.21
  118.2 3.0 collective-permute-start.7
  121.3 1.6 collective-permute-done.8
  122.9 2.7 fusion.36
  125.6 2.7 collective-permute-start.9
  128.7 9.0 %collective-permute-done.9 = bf16[128,1792]{1,0:T(8,128)(2,1)S(1)} collective-permute-done((bf16[128,1792]{1,0:T(8,128)(2,1)S(1)}, bf16[128,1792]{1,0:T(8,128)(2,1)S(1)}, u32[]{:S(2)}, u32[]{:S(2)}) %collective-permute-start.9) | collective-permute-done | bytes 458784 | tf_op jit(solution)/shard_map/ppermute | solution.py:36
  137.9 1.7 fusion.53
  140.0 2.3 collective-permute-start.11
  142.3 1.9 fusion.1
  144.2 7.2 %all-to-all-start.2 = ((bf16[32,8,3584]{2,1,0:T(8,128)(2,1)}), bf16[32,8,3584]{2,1,0:T(8,128)(2,1)S(1)}, u32[]{:S(2)}, u32[]{:S(2)}) async-start(bf16[32,8,3584]{2,1,0:T(8,128)(2,1)} %fusion.1), calls=%async_computation.2 | async-start | bytes 3670016 | tf_op jit(solution)/shard_map/all_to_all | solution.py:40
  151.5 11.5 %collective-permute-done.10 = bf16[128,3584]{1,0:T(8,128)(2,1)} collective-permute-done((bf16[128,3584]{1,0:T(8,128)(2,1)S(1)}, bf16[128,3584]{1,0:T(8,128)(2,1)}, u32[]{:S(2)}, u32[]{:S(2)}) %collective-permute-start.10) | collective-permute-done | bytes 917536 | tf_op jit(solution)/shard_map/ppermute | solution.py:32
  163.0 1.5 fusion.52
  164.5 1.6 fusion.45
  166.1 4.0 %convolution_convert_fusion = bf16[768,3584]{1,0:T(8,128)(2,1)} fusion(bf16[128,3584]{1,0:T(8,128)(2,1)S(1)} %get-tuple-element.83, bf16[128,3584]{1,0:T(8,128)(2,1)S(1)} %get-tuple-element.82, pred[768,128]{1,0:T(8,128)(4,1)S(1)} %bitcast.124, pred[768,128]{1,0:T(8,128)(4,1)S(1)} %bitcast.123), kind=kOutput, calls=%fused_computation.2 | convolution fusion | flops 1415905280 | bytes 7536640 | tf_op jit(solution)/shard_map/dot_general | solution.py:24
  170.1 10.3 %collective-permute-done.11 = bf16[272,1792]{1,0:T(8,128)(2,1)} collective-permute-done((bf16[272,1792]{1,0:T(8,128)(2,1)}, bf16[272,1792]{1,0:T(8,128)(2,1)}, u32[]{:S(2)}, u32[]{:S(2)}) %collective-permute-start.11) | collective-permute-done | bytes 974880 | tf_op jit(solution)/shard_map/ppermute | solution.py:32
  181.6 7.8 %all-to-all-start.3 = ((bf16[32,24,3584]{2,1,0:T(8,128)(2,1)}), bf16[32,24,3584]{2,1,0:T(8,128)(2,1)}, u32[]{:S(2)}, u32[]{:S(2)}) async-start(bf16[32,24,3584]{2,1,0:T(8,128)(2,1)} %bitcast.111), calls=%async_computation.3 | async-start | bytes 11010048 | tf_op jit(solution)/shard_map/all_to_all | solution.py:40
  190.0 3.1 copy-done.2
  193.1 3.1 copy-done.4
  196.1 1.5 copy-done.12
  197.6 3.1 shard_map.118
  200.7 31.1 %collective-permute-done.12.x_ref = bf16[256,3584]{1,0:T(8,128)(2,1)S(1)} collective-permute-done((bf16[256,3584]{1,0:T(8,128)(2,1)}, bf16[256,3584]{1,0:T(8,128)(2,1)S(1)}, u32[]{:S(2)}, u32[]{:S(2)}) %collective-permute-start.12) | collective-permute-done | bytes 1835040 | tf_op jit(solution)/shard_map/ppermute | solution.py:32
  231.8 3.2 copy-done.5
  235.1 3.3 shard_map.119.mine_ref
  238.8 1.4 constant_dynamic-update-slice_fusion.3
  241.4 4.8 %collective-permute-done.13.theirs_ref = bf16[256,512]{1,0:T(8,128)(2,1)S(1)} collective-permute-done((bf16[256,512]{1,0:T(8,128)(2,1)S(1)}, bf16[256,512]{1,0:T(8,128)(2,1)S(1)}, u32[]{:S(2)}, u32[]{:S(2)}) %collective-permute-start.13) | collective-permute-done | bytes 262176 | tf_op jit(solution)/shard_map/ppermute | solution.py:32
  246.2 4.5 %shard_map.120 = bf16[512,1792]{1,0:T(8,128)(2,1)S(1)} custom-call(s32[4]{0:T(128)S(1)} %pad_add_fusion.4.order_ref, bf16[256,512]{1,0:T(8,128)(2,1)S(1)} %shard_map.119.mine_ref, bf16[256,512]{1,0:T(8,128)(2,1)S(1)} %collective-permute-done.13.theirs_ref, bf16[256,256]{1,0:T(8,128)(2,1)S(1)} %fusion.76.place_ref, bf16[1,512,7168]{2,1,0:T(8,128)(2,1)S(1)} %bitcast.102, ...), custom_call_target="tpu_custom_call" | custom-call | flops 1000 | bytes 1000 | tf_op jit(solution)/shard_map/pallas_call | solution.py:126
  252.0 5.9 %all-to-all-done.3 = bf16[32,24,3584]{2,1,0:T(8,128)(2,1)} async-done(((bf16[32,24,3584]{2,1,0:T(8,128)(2,1)}), bf16[32,24,3584]{2,1,0:T(8,128)(2,1)}, u32[]{:S(2)}, u32[]{:S(2)}) %all-to-all-start.3) | async-done | bytes 5505056 | tf_op jit(solution)/shard_map/all_to_all | solution.py:40
  257.9 10.2 %all-to-all-start.4 = ((bf16[32,16,1792]{2,1,0:T(8,128)(2,1)}), bf16[32,16,1792]{2,1,0:T(8,128)(2,1)}, u32[]{:S(2)}, u32[]{:S(2)}) async-start(bf16[32,16,1792]{2,1,0:T(8,128)(2,1)} %bitcast.106), calls=%async_computation.4 | async-start | bytes 3670016 | tf_op jit(solution)/shard_map/all_to_all | solution.py:40
  268.3 3.1 copy-done.3
  271.4 12.1 %shard_map.121.mine_ref = bf16[384,512]{1,0:T(8,128)(2,1)S(1)} custom-call(s32[4]{0:T(128)S(1)} %pad_add_fusion.4.order_ref, bf16[768,3584]{1,0:T(8,128)(2,1)} %bitcast.31.x_ref, bf16[192,192]{1,0:T(8,128)(2,1)S(1)} %get-tuple-element.81.pick_ref, bf16[1,7168,512]{2,1,0:T(8,128)(2,1)S(1)} %copy-done.3, bf16[1,7168,512]{2,1,0:T(8,128)(2,1)} %wu_ref.5), custom_call_target="tpu_custom_call" | custom-call | flops 1000 | bytes 1000 | tf_op jit(solution)/shard_map/pallas_call | solution.py:126
  284.1 10.9 %collective-permute-done.14.theirs_ref = bf16[384,512]{1,0:T(8,128)(2,1)S(1)} collective-permute-done((bf16[384,512]{1,0:T(8,128)(2,1)S(1)}, bf16[384,512]{1,0:T(8,128)(2,1)S(1)}, u32[]{:S(2)}, u32[]{:S(2)}) %collective-permute-start.14) | collective-permute-done | bytes 393248 | tf_op jit(solution)/shard_map/ppermute | solution.py:32
  295.0 6.7 %shard_map.122 = bf16[768,1792]{1,0:T(8,128)(2,1)S(1)} custom-call(s32[4]{0:T(128)S(1)} %pad_add_fusion.4.order_ref, bf16[384,512]{1,0:T(8,128)(2,1)S(1)} %shard_map.121.mine_ref, bf16[384,512]{1,0:T(8,128)(2,1)S(1)} %collective-permute-done.14.theirs_ref, bf16[192,192]{1,0:T(8,128)(2,1)S(1)} %get-tuple-element.80.place_ref, bf16[1,512,7168]{2,1,0:T(8,128)(2,1)} %refs_1_.3, ...), custom_call_target="tpu_custom_call" | custom-call | flops 1000 | bytes 1000 | tf_op jit(solution)/shard_map/pallas_call | solution.py:126
  301.7 1.5 copy-done.6
  303.3 7.4 %all-to-all-start.5 = ((bf16[32,24,1792]{2,1,0:T(8,128)(2,1)}), bf16[32,24,1792]{2,1,0:T(8,128)(2,1)S(1)}, u32[]{:S(2)}, u32[]{:S(2)}) async-start(bf16[32,24,1792]{2,1,0:T(8,128)(2,1)} %bitcast.105), calls=%async_computation.5 | async-start | bytes 5505024 | tf_op jit(solution)/shard_map/all_to_all | solution.py:40
  311.1 3.0 fusion.149
  314.1 2.9 convolution_add_fusion.2
  317.0 29.7 %all-to-all-done.5 = bf16[32,24,1792]{2,1,0:T(8,128)(2,1)S(1)} async-done(((bf16[32,24,1792]{2,1,0:T(8,128)(2,1)}), bf16[32,24,1792]{2,1,0:T(8,128)(2,1)S(1)}, u32[]{:S(2)}, u32[]{:S(2)}) %all-to-all-start.5) | async-done | bytes 2752544 | tf_op jit(solution)/shard_map/all_to_all | solution.py:40
  346.7 1.8 fusion.11
  348.5 3.3 collective-permute-start.15
  351.8 10.2 %collective-permute-done.15 = bf16[128,1792]{1,0:T(8,128)(2,1)S(1)} collective-permute-done((bf16[128,1792]{1,0:T(8,128)(2,1)S(1)}, bf16[128,1792]{1,0:T(8,128)(2,1)S(1)}, u32[]{:S(2)}, u32[]{:S(2)}) %collective-permute-start.15) | collective-permute-done | bytes 458784 | tf_op jit(solution)/shard_map/ppermute | solution.py:36
  362.1 1.3 add_convert_fusion
  (135 shorter events, 22.9 us)
Async XLA Ops:
  6.5 74.1 %copy-start = (bf16[128,1024]{1,0:T(8,128)(2,1)S(1)}, bf16[128,1024]{1,0:T(8,128)(2,1)}, u32[]{:S(2)}) copy-start(bf16[128,1024]{1,0:T(8,128)(2,1)} %param.12) | copy-start | bytes 786436
  6.5 20.5 %copy-start.23 = (s32[32,3]{0,1:T(4,128)S(1)}, s32[32,3]{0,1:T(4,128)}, u32[]{:S(2)}) copy-start(s32[32,3]{0,1:T(4,128)} %param.15) | copy-start | bytes 1156
  6.5 92.0 %all-gather.2.cloned.1.call-start = ((), (), s32[]{:S(2)}) async-start(), calls=%async_computation.6 | async-start | bytes 15138816 | tf_op jit(solution)/shard_map/all_gather | solution.py:359
  9.2 24.4 %collective-permute-start.1 = (bf16[1,1792]{1,0:T(2,128)(2,1)S(1)}, bf16[1,1792]{1,0:T(2,128)(2,1)S(1)}, u32[]{:S(2)}, u32[]{:S(2)}) collective-permute-start(bf16[1,1792]{1,0:T(2,128)(2,1)S(1)} %broadcast_in_dim.131), channel_id=1, source_target_pairs={{0,3},{1,2},{2,1},{3,0},{4,7},{5,6},{6,5},{7,4},{8,11},{9,10},{10,... | collective-permute-start | bytes 10760 | tf_op jit(solution)/shard_map/ppermute | solution.py:36
  16.7 37.5 %collective-permute-start = (bf16[256,1024]{1,0:T(8,128)(2,1)}, bf16[256,1024]{1,0:T(8,128)(2,1)}, u32[]{:S(2)}, u32[]{:S(2)}) collective-permute-start(bf16[256,1024]{1,0:T(8,128)(2,1)} %constant_dynamic-update-slice_fusion), channel_id=1, source_target_pairs={{0,4},{4,8},{8,12},{12,16},{16,20},{20,24},{24,28},{28,32},{32,36}... | collective-permute-start | bytes 1572872 | tf_op jit(solution)/shard_map/ppermute | solution.py:49
  18.9 22.8 %all-to-all-start = ((bf16[32,8,1024]{2,1,0:T(8,128)(2,1)}), bf16[32,8,1024]{2,1,0:T(8,128)(2,1)S(1)}, u32[]{:S(2)}, u32[]{:S(2)}) async-start(bf16[32,8,1024]{2,1,0:T(8,128)(2,1)} %bitcast.13), calls=%async_computation | async-start | bytes 1048576 | tf_op jit(solution)/shard_map/all_to_all | solution.py:40
  26.9 25.0 %collective-permute-start.5 = (bf16[128,1792]{1,0:T(8,128)(2,1)}, bf16[128,1792]{1,0:T(8,128)(2,1)}, u32[]{:S(2)}, u32[]{:S(2)}) collective-permute-start(bf16[128,1792]{1,0:T(8,128)(2,1)} %param.16), channel_id=1, source_target_pairs={{0,3},{1,2},{2,1},{3,0},{4,7},{5,6},{6,5},{7,4},{8,11},{9,10},{10,... | collective-permute-start | bytes 1376264 | tf_op jit(solution)/shard_map/ppermute | solution.py:36
  29.9 3.7 copy-start.21
  30.0 3.9 %copy-start.17 = (bf16[128,1024]{1,0:T(8,128)(2,1)S(1)}, bf16[128,1024]{1,0:T(8,128)(2,1)}, u32[]{:S(2)}) copy-start(bf16[128,1024]{1,0:T(8,128)(2,1)} %param.13) | copy-start | bytes 786436
  30.0 4.1 %copy-start.18 = (bf16[128,1024]{1,0:T(8,128)(2,1)S(1)}, bf16[128,1024]{1,0:T(8,128)(2,1)}, u32[]{:S(2)}) copy-start(bf16[128,1024]{1,0:T(8,128)(2,1)} %param.14) | copy-start | bytes 786436
  33.6 4.9 %copy-start.13 = (bf16[512,1792]{1,0:T(8,128)(2,1)}, bf16[512,1792]{1,0:T(8,128)(2,1)S(1)}, u32[]{:S(2)}) copy-start(bf16[512,1792]{1,0:T(8,128)(2,1)S(1)} %get-tuple-element.32) | copy-start | bytes 5505028
  33.7 3.8 %collective-permute-start.2 = (bf16[1,3584]{1,0:T(2,128)(2,1)S(1)}, bf16[1,3584]{1,0:T(2,128)(2,1)S(1)}, u32[]{:S(2)}, u32[]{:S(2)}) collective-permute-start(bf16[1,3584]{1,0:T(2,128)(2,1)S(1)} %pad_maximum_fusion.1.gain_ref), channel_id=1, source_target_pairs={{0,1},{1,0},{2,3},{3,2},{4,5},{5,4},{6,7},{7,6},{8,9},{9,8},{10,11... | collective-permute-start | bytes 21512 | tf_op jit(solution)/shard_map/ppermute | solution.py:32
  38.5 48.6 %collective-permute-start.4 = (bf16[240,1792]{1,0:T(8,128)(2,1)}, bf16[240,1792]{1,0:T(8,128)(2,1)}, u32[]{:S(2)}, u32[]{:S(2)}) collective-permute-start(bf16[240,1792]{1,0:T(8,128)(2,1)} %slice.53), channel_id=1, source_target_pairs={{0,1},{1,0},{2,3},{3,2},{4,5},{5,4},{6,7},{7,6},{8,9},{9,8},{10,11... | collective-permute-start | bytes 2580488 | tf_op jit(solution)/shard_map/ppermute | solution.py:32
  38.8 59.8 %collective-permute-start.3 = (bf16[512,1792]{1,0:T(8,128)(2,1)}, bf16[512,1792]{1,0:T(8,128)(2,1)S(1)}, u32[]{:S(2)}, u32[]{:S(2)}) collective-permute-start(bf16[512,1792]{1,0:T(8,128)(2,1)} %get-tuple-element.31), channel_id=1, source_target_pairs={{0,1},{1,0},{2,3},{3,2},{4,5},{5,4},{6,7},{7,6},{8,9},{9,8},{10,11... | collective-permute-start | bytes 5505032 | tf_op jit(solution)/shard_map/ppermute | solution.py:32
  45.6 33.4 %all-to-all-start.1 = ((bf16[32,16,1024]{2,1,0:T(8,128)(2,1)}), bf16[32,16,1024]{2,1,0:T(8,128)(2,1)S(1)}, u32[]{:S(2)}, u32[]{:S(2)}) async-start(bf16[32,16,1024]{2,1,0:T(8,128)(2,1)} %bitcast_select_fusion.2), calls=%async_computation.1 | async-start | bytes 2097152 | tf_op jit(solution)/shard_map/all_to_all | solution.py:40
  80.6 3.2 copy-start.19
  80.6 3.2 copy-start.20
  98.6 3.4 copy-start.7
  101.9 13.5 %collective-permute-start.6 = (bf16[128,1792]{1,0:T(8,128)(2,1)S(1)}, bf16[128,1792]{1,0:T(8,128)(2,1)S(1)}, u32[]{:S(2)}, u32[]{:S(2)}) collective-permute-start(bf16[128,1792]{1,0:T(8,128)(2,1)S(1)} %fusion.24), channel_id=1, source_target_pairs={{0,1},{1,0},{2,3},{3,2},{4,5},{5,4},{6,7},{7,6},{8,9},{9,8},{10,11... | collective-permute-start | bytes 1376264 | tf_op jit(solution)/shard_map/ppermute | solution.py:32
  107.8 13.3 %copy-start.22 = (s32[128,8]{0,1:T(8,128)S(1)}, s32[128,8]{0,1:T(8,128)}, u32[]{:S(2)}) copy-start(s32[128,8]{0,1:T(8,128)} %param.22) | copy-start | bytes 12292
  107.8 15.0 %collective-permute-start.8 = (bf16[128,1792]{1,0:T(8,128)(2,1)S(1)}, bf16[128,1792]{1,0:T(8,128)(2,1)S(1)}, u32[]{:S(2)}, u32[]{:S(2)}) collective-permute-start(bf16[128,1792]{1,0:T(8,128)(2,1)S(1)} %fusion.39), channel_id=1, source_target_pairs={{0,1},{1,0},{2,3},{3,2},{4,5},{5,4},{6,7},{7,6},{8,9},{9,8},{10,11... | collective-permute-start | bytes 1376264 | tf_op jit(solution)/shard_map/ppermute | solution.py:32
  118.2 10.5 %collective-permute-start.7 = (bf16[128,1792]{1,0:T(8,128)(2,1)S(1)}, bf16[128,1792]{1,0:T(8,128)(2,1)S(1)}, u32[]{:S(2)}, u32[]{:S(2)}) collective-permute-start(bf16[128,1792]{1,0:T(8,128)(2,1)S(1)} %fusion.21), channel_id=1, source_target_pairs={{0,3},{1,2},{2,1},{3,0},{4,7},{5,6},{6,5},{7,4},{8,11},{9,10},{10,... | collective-permute-start | bytes 1376264 | tf_op jit(solution)/shard_map/ppermute | solution.py:36
  125.6 12.3 %copy-start.16 = (bf16[128,3584]{1,0:T(8,128)(2,1)S(1)}, bf16[128,3584]{1,0:T(8,128)(2,1)}, u32[]{:S(2)}) copy-start(bf16[128,3584]{1,0:T(8,128)(2,1)} %pad_maximum_fusion) | copy-start | bytes 2752516
  125.6 12.2 %collective-permute-start.9 = (bf16[128,1792]{1,0:T(8,128)(2,1)S(1)}, bf16[128,1792]{1,0:T(8,128)(2,1)S(1)}, u32[]{:S(2)}, u32[]{:S(2)}) collective-permute-start(bf16[128,1792]{1,0:T(8,128)(2,1)S(1)} %fusion.36), channel_id=1, source_target_pairs={{0,3},{1,2},{2,1},{3,0},{4,7},{5,6},{6,5},{7,4},{8,11},{9,10},{10,... | collective-permute-start | bytes 1376264 | tf_op jit(solution)/shard_map/ppermute | solution.py:36
  139.6 23.4 %collective-permute-start.10 = (bf16[128,3584]{1,0:T(8,128)(2,1)S(1)}, bf16[128,3584]{1,0:T(8,128)(2,1)}, u32[]{:S(2)}, u32[]{:S(2)}) collective-permute-start(bf16[128,3584]{1,0:T(8,128)(2,1)S(1)} %get-tuple-element.56), channel_id=1, source_target_pairs={{0,1},{1,0},{2,3},{3,2},{4,5},{5,4},{6,7},{7,6},{8,9},{9,8},{10,11... | collective-permute-start | bytes 2752520 | tf_op jit(solution)/shard_map/ppermute | solution.py:32
  140.0 40.4 %collective-permute-start.11 = (bf16[272,1792]{1,0:T(8,128)(2,1)}, bf16[272,1792]{1,0:T(8,128)(2,1)}, u32[]{:S(2)}, u32[]{:S(2)}) collective-permute-start(bf16[272,1792]{1,0:T(8,128)(2,1)} %slice.54), channel_id=1, source_target_pairs={{0,1},{1,0},{2,3},{3,2},{4,5},{5,4},{6,7},{7,6},{8,9},{9,8},{10,11... | collective-permute-start | bytes 2924552 | tf_op jit(solution)/shard_map/ppermute | solution.py:32
  144.2 36.2 %all-to-all-start.2 = ((bf16[32,8,3584]{2,1,0:T(8,128)(2,1)}), bf16[32,8,3584]{2,1,0:T(8,128)(2,1)S(1)}, u32[]{:S(2)}, u32[]{:S(2)}) async-start(bf16[32,8,3584]{2,1,0:T(8,128)(2,1)} %fusion.1), calls=%async_computation.2 | async-start | bytes 3670016 | tf_op jit(solution)/shard_map/all_to_all | solution.py:40
  180.4 1.2 copy-start.11
  181.6 50.2 %slice-start.2 = ((s8[7340032]{0:T(1024)(128)(4,1)}), s8[3145728]{0:T(1024)(128)(4,1)S(1)}, s32[]{:S(2)}) async-start(s8[7340032]{0:T(1024)(128)(4,1)} %bitcast.103), calls=%async_computation.9 | async-start | bytes 6291456
  181.6 76.2 %all-to-all-start.3 = ((bf16[32,24,3584]{2,1,0:T(8,128)(2,1)}), bf16[32,24,3584]{2,1,0:T(8,128)(2,1)}, u32[]{:S(2)}, u32[]{:S(2)}) async-start(bf16[32,24,3584]{2,1,0:T(8,128)(2,1)} %bitcast.111), calls=%async_computation.3 | async-start | bytes 11010048 | tf_op jit(solution)/shard_map/all_to_all | solution.py:40
  189.4 42.4 %collective-permute-start.12 = (bf16[256,3584]{1,0:T(8,128)(2,1)}, bf16[256,3584]{1,0:T(8,128)(2,1)S(1)}, u32[]{:S(2)}, u32[]{:S(2)}) collective-permute-start(bf16[256,3584]{1,0:T(8,128)(2,1)} %bitcast.107), channel_id=1, source_target_pairs={{0,1},{1,0},{2,3},{3,2},{4,5},{5,4},{6,7},{7,6},{8,9},{9,8},{10,11... | collective-permute-start | bytes 5505032 | tf_op jit(solution)/shard_map/ppermute | solution.py:32
  190.0 3.1 copy-start.2
  193.1 3.1 copy-start.4
  196.1 1.5 copy-start.12
  197.6 34.2 %slice-start.3 = ((s8[7340032]{0:T(1024)(128)(4,1)}), s8[4194304]{0:T(1024)(128)(4,1)S(1)}, s32[]{:S(2)}) async-start(s8[7340032]{0:T(1024)(128)(4,1)} %bitcast.103), calls=%async_computation.10 | async-start | bytes 8388608
  231.8 14.4 %slice-start = ((s8[7340032]{0:T(1024)(128)(4,1)}), s8[4194304]{0:T(1024)(128)(4,1)S(1)}, s32[]{:S(2)}) async-start(s8[7340032]{0:T(1024)(128)(4,1)} %bitcast.101), calls=%async_computation.7 | async-start | bytes 8388608
  231.8 3.2 copy-start.5
  235.1 11.1 %slice-start.1 = ((s8[7340032]{0:T(1024)(128)(4,1)}), s8[3145728]{0:T(1024)(128)(4,1)S(1)}, s32[]{:S(2)}) async-start(s8[7340032]{0:T(1024)(128)(4,1)} %bitcast.101), calls=%async_computation.8 | async-start | bytes 6291456
  238.4 7.8 %copy-start.8 = (bf16[512,1792]{1,0:T(8,128)(2,1)S(1)}, bf16[512,1792]{1,0:T(8,128)(2,1)}, u32[]{:S(2)}) copy-start(bf16[512,1792]{1,0:T(8,128)(2,1)} %copy-done.7) | copy-start | bytes 5505028
  238.4 7.8 %collective-permute-start.13 = (bf16[256,512]{1,0:T(8,128)(2,1)S(1)}, bf16[256,512]{1,0:T(8,128)(2,1)S(1)}, u32[]{:S(2)}, u32[]{:S(2)}) collective-permute-start(bf16[256,512]{1,0:T(8,128)(2,1)S(1)} %shard_map.119.mine_ref), channel_id=1, source_target_pairs={{0,1},{1,0},{2,3},{3,2},{4,5},{5,4},{6,7},{7,6},{8,9},{9,8},{10,11... | collective-permute-start | bytes 786440 | tf_op jit(solution)/shard_map/ppermute | solution.py:32
  250.8 1.3 copy-start.10
  257.9 45.4 %all-to-all-start.4 = ((bf16[32,16,1792]{2,1,0:T(8,128)(2,1)}), bf16[32,16,1792]{2,1,0:T(8,128)(2,1)}, u32[]{:S(2)}, u32[]{:S(2)}) async-start(bf16[32,16,1792]{2,1,0:T(8,128)(2,1)} %bitcast.106), calls=%async_computation.4 | async-start | bytes 3670016 | tf_op jit(solution)/shard_map/all_to_all | solution.py:40
  268.3 3.1 copy-start.3
  271.4 23.7 %copy-start.9 = (bf16[512,1792]{1,0:T(8,128)(2,1)S(1)}, bf16[512,1792]{1,0:T(8,128)(2,1)}, u32[]{:S(2)}) copy-start(bf16[512,1792]{1,0:T(8,128)(2,1)} %copy-done.7) | copy-start | bytes 5505028
  283.5 11.5 %collective-permute-start.14 = (bf16[384,512]{1,0:T(8,128)(2,1)S(1)}, bf16[384,512]{1,0:T(8,128)(2,1)S(1)}, u32[]{:S(2)}, u32[]{:S(2)}) collective-permute-start(bf16[384,512]{1,0:T(8,128)(2,1)S(1)} %shard_map.121.mine_ref), channel_id=1, source_target_pairs={{0,1},{1,0},{2,3},{3,2},{4,5},{5,4},{6,7},{7,6},{8,9},{9,8},{10,11... | collective-permute-start | bytes 1179656 | tf_op jit(solution)/shard_map/ppermute | solution.py:32
  301.7 1.5 copy-start.6
  303.3 7.4 %copy-start.24 = (bf16[128,8]{0,1:T(8,128)(2,1)S(1)}, bf16[128,8]{0,1:T(8,128)(2,1)}, u32[]{:S(2)}) copy-start(bf16[128,8]{0,1:T(8,128)(2,1)} %param.23) | copy-start | bytes 6148
  303.3 43.4 %all-to-all-start.5 = ((bf16[32,24,1792]{2,1,0:T(8,128)(2,1)}), bf16[32,24,1792]{2,1,0:T(8,128)(2,1)S(1)}, u32[]{:S(2)}, u32[]{:S(2)}) async-start(bf16[32,24,1792]{2,1,0:T(8,128)(2,1)} %bitcast.105), calls=%async_computation.5 | async-start | bytes 5505024 | tf_op jit(solution)/shard_map/all_to_all | solution.py:40
  310.7 3.4 copy-start.14
  346.7 15.4 %copy-start.15 = (f32[128,1792]{1,0:T(8,128)S(1)}, f32[128,1792]{1,0:T(8,128)}, u32[]{:S(2)}) copy-start(f32[128,1792]{1,0:T(8,128)} %convolution_add_fusion.2) | copy-start | bytes 2752516
  346.7 16.7 %copy-start.1 = (bf16[128,1024]{1,0:T(8,128)(2,1)S(1)}, bf16[128,1024]{1,0:T(8,128)(2,1)}, u32[]{:S(2)}) copy-start(bf16[128,1024]{1,0:T(8,128)(2,1)} %param.12) | copy-start | bytes 786436
  348.5 13.5 %collective-permute-start.15 = (bf16[128,1792]{1,0:T(8,128)(2,1)S(1)}, bf16[128,1792]{1,0:T(8,128)(2,1)S(1)}, u32[]{:S(2)}, u32[]{:S(2)}) collective-permute-start(bf16[128,1792]{1,0:T(8,128)(2,1)S(1)} %fusion.11), channel_id=1, source_target_pairs={{0,3},{1,2},{2,1},{3,0},{4,7},{5,6},{6,5},{7,4},{8,11},{9,10},{10,... | collective-permute-start | bytes 1376264 | tf_op jit(solution)/shard_map/ppermute | solution.py:36
Sparse Core Ops, SparseCore 0:
  9.6 85.4 all-gather.1
where the time goes:
time: 372 us; the launch traced here: 370 us
  waiting for transfers between devices  165 us (44%)
  starting transfers between devices  70.1 us (19%)
  local copies, waits for them, and re-layouts  45.2 us (12%)
  matrix products  33 us (9%)
  Pallas kernels  29.7 us (8%)
  between operations  14 us (4%)
  other arithmetic  12.8 us (3%)
    ppermute x10, waiting for transfers between devices, half_swap(): return lax.ppermute(block, 'exp', [(i, i ^ 1) for i in range(4)])  89.6 us
    all_to_all x6, waiting for transfers between devices, spread(): return lax.all_to_all(block, 'seq', split_axis=0, concat_axis=0, tiled=True)  56 us
    all_to_all x6, starting transfers between devices, spread(): return lax.all_to_all(block, 'seq', split_axis=0, concat_axis=0, tiled=True)  46.8 us
    pallas_call x5, Pallas kernels, call(): pl.pallas_call(kernel, grid_spec=pltpu.PrefetchScalarGridSpec(num_scalar_...  29.7 us
    unnamed x64, local copies, waits for them, and re-layouts  22.4 us
    ppermute x5, waiting for transfers between devices, group_swap(): return lax.ppermute(block, 'exp', [(i, 3 - i) for i in range(4)])  19.6 us
    dot_general x8, matrix products, dot(): return jnp.dot(a, b, preferred_element_type=F32)  18.4 us
    ppermute x5, starting transfers between devices, group_swap(): return lax.ppermute(block, 'exp', [(i, 3 - i) for i in range(4)])  13.2 us
  transfers between devices with their start and end apart: 23, of which 16 were waited for; matrix products, arithmetic and copies ran while one was open for 17% of the time, Pallas kernels for 8%

commit v1 on v0

--- a/solution.py
+++ b/solution.py
@@ -12,7 +12,8 @@
 CAP = 20
 DIRECT = 12
 SWAPPED = CAP - DIRECT
-EARLY = 240
+EARLY = 208
+MIDDLE = 320
 STEP = 1792
 OUT_STEP = 896
 MIB = 2**20
@@ -105,6 +106,8 @@
 
     given = [half_swap(product(theirs_order[n])) for n in range(2)]
     kept = [product(order[n]) for n in range(2)]
+    for n in range(2):
+        given[n], kept[n] = lax.optimization_barrier((given[n], kept[n]))
     given[0], behind = lax.optimization_barrier((given[0], behind))
     pairs = [(a.astype(F32) + b.astype(F32)).astype(BF16) for a, b in zip(kept, given)]
     total = [pair.astype(F32) + group_swap(pair).astype(F32) for pair in pairs]
@@ -405,13 +408,15 @@
 
     attended = attend(query_states, key_states, value_states, selected, heads)
     attended = regroup(attended, heads, count)
-    attended, early, residual_half = lax.optimization_barrier((attended, early, residual_half))
-    total, late = project_sum(
-        attended, full_out, order, theirs_order, width, down_given[1][EARLY:]
-    )
-    late = half_swap(late)
+    late = [down_given[1][EARLY:MIDDLE], down_given[1][MIDDLE:]]
+    attended, early, late, residual_half = lax.optimization_barrier(
+        (attended, early, late, residual_half)
+    )
+    total, late = project_sum(attended, full_out, order, theirs_order, width, late)
+    late = [half_swap(block) for block in late]
     hidden = (total + residual_half.astype(F32)).astype(BF16).astype(F32)
     gained = (hidden * gain_mine.astype(F32)).astype(BF16)
+    gained, late[0] = lax.optimization_barrier((gained, late[0]))
     gained_other = half_swap(gained)
 
     received = spread(dot(picker(first), gained).astype(BF16))
@@ -423,8 +428,8 @@
     scale = lax.rsqrt(squares / model_width + EPSILON)
     both = jnp.concatenate([(block.astype(F32) * scale).astype(BF16) for block, _ in halves], axis=0)
     rows_out = dot(pick_last, both).astype(BF16)
-    rows_out, received, late = lax.optimization_barrier((rows_out, received, late))
-    down_theirs = [early[0], jnp.concatenate([early[1], late], axis=0)]
+    rows_out, received, late[1] = lax.optimization_barrier((rows_out, received, late[1]))
+    down_theirs = [early[0], jnp.concatenate([early[1], *late], axis=0)]
     received_last = spread(rows_out)
 
     before = half_units(received, gain_mine, order, w_gate, w_up)

time: 372 us -> 365 us (0.981)
  waiting for transfers between devices: 165 us -> 158 us
  starting transfers between devices: 70.1 us -> 66.3 us
    ppermute x10 -> x11, waiting for transfers between devices: 89.6 us -> 81.7 us  [half_swap(): return lax.ppermute(block, 'exp', [(i, i ^ 1) for i in range(4)])]
    unnamed x64 -> x81, local copies, waits for them, and re-layouts: 22.4 us -> 23.2 us
    ppermute x10 -> x11, starting transfers between devices: 7.9 us -> 7.2 us  [half_swap(): return lax.ppermute(block, 'exp', [(i, i ^ 1) for i in range(4)])]
  transfers between devices with their start and end apart: 23 -> 24, of which waited for: 16 -> 16; matrix products, arithmetic and copies ran while one was open for 17% -> 18% of each run, Pallas kernels for 8% -> 8%
where the time goes in v1:
time: 365 us; the launch traced here: 363 us
  waiting for transfers between devices  158 us (43%)
  starting transfers between devices  66.3 us (18%)
  local copies, waits for them, and re-layouts  46.3 us (13%)
  matrix products  33 us (9%)
  Pallas kernels  30.7 us (8%)
  other arithmetic  14.5 us (4%)
  between operations  14.1 us (4%)
    ppermute x11, waiting for transfers between devices, half_swap(): return lax.ppermute(block, 'exp', [(i, i ^ 1) for i in range(4)])  81.7 us
    all_to_all x6, waiting for transfers between devices, spread(): return lax.all_to_all(block, 'seq', split_axis=0, concat_axis=0, tiled=True)  56.7 us
    all_to_all x6, starting transfers between devices, spread(): return lax.all_to_all(block, 'seq', split_axis=0, concat_axis=0, tiled=True)  44.3 us
    pallas_call x5, Pallas kernels, call(): pl.pallas_call(kernel, grid_spec=pltpu.PrefetchScalarGridSpec(num_scalar_...  30.7 us
    unnamed x81, local copies, waits for them, and re-layouts  23.2 us
    ppermute x5, waiting for transfers between devices, group_swap(): return lax.ppermute(block, 'exp', [(i, 3 - i) for i in range(4)])  20 us
    dot_general x8, matrix products, dot(): return jnp.dot(a, b, preferred_element_type=F32)  18.4 us
    ppermute x5, starting transfers between devices, group_swap(): return lax.ppermute(block, 'exp', [(i, 3 - i) for i in range(4)])  12.5 us
  transfers between devices with their start and end apart: 24, of which 16 were waited for; matrix products, arithmetic and copies ran while one was open for 18% of the time, Pallas kernels for 8%

profile of v1, /device:TPU:0, one launch (start us, length us, event | category | flops | bytes accessed | tf_op | source)
XLA Modules:
  0.0 363.3 jit_solution(16235060792720953559)
XLA Ops:
  6.5 1.9 reshape.220
  9.2 4.1 %collective-permute-start.1 = (bf16[1,1792]{1,0:T(2,128)(2,1)S(1)}, bf16[1,1792]{1,0:T(2,128)(2,1)S(1)}, u32[]{:S(2)}, u32[]{:S(2)}) collective-permute-start(bf16[1,1792]{1,0:T(2,128)(2,1)S(1)} %broadcast_in_dim.131), channel_id=1, source_target_pairs={{0,3},{1,2},{2,1},{3,0},{4,7},{5,6},{6,5},{7,4},{8,11},{9,10},{10,... | collective-permute-start | bytes 10760 | tf_op jit(solution)/shard_map/ppermute | solution.py:37
  13.3 1.7 constant_dynamic-update-slice_fusion.1
  15.0 1.7 constant_dynamic-update-slice_fusion
  16.7 2.3 collective-permute-start
  18.9 8.0 %all-to-all-start = ((bf16[32,8,1024]{2,1,0:T(8,128)(2,1)}), bf16[32,8,1024]{2,1,0:T(8,128)(2,1)S(1)}, u32[]{:S(2)}, u32[]{:S(2)}) async-start(bf16[32,8,1024]{2,1,0:T(8,128)(2,1)} %bitcast.13), calls=%async_computation | async-start | bytes 1048576 | tf_op jit(solution)/shard_map/all_to_all | solution.py:41
  28.6 1.3 compare_select_fusion.5
  31.0 3.6 dynamic-slice_bitcast_fusion
  37.5 3.7 %collective-permute-done.2.gain_ref = bf16[1,3584]{1,0:T(2,128)(2,1)S(1)} collective-permute-done((bf16[1,3584]{1,0:T(2,128)(2,1)S(1)}, bf16[1,3584]{1,0:T(2,128)(2,1)S(1)}, u32[]{:S(2)}, u32[]{:S(2)}) %collective-permute-start.2) | collective-permute-done | bytes 7200 | tf_op jit(solution)/shard_map/ppermute | solution.py:33
  43.8 2.0 collective-permute-start.3
  45.8 1.6 gather_fusion
  47.4 2.4 bitcast_select_fusion.2
  49.8 7.4 %all-to-all-start.1 = ((bf16[32,16,1024]{2,1,0:T(8,128)(2,1)}), bf16[32,16,1024]{2,1,0:T(8,128)(2,1)S(1)}, u32[]{:S(2)}, u32[]{:S(2)}) async-start(bf16[32,16,1024]{2,1,0:T(8,128)(2,1)} %bitcast_select_fusion.2), calls=%async_computation.1 | async-start | bytes 2097152 | tf_op jit(solution)/shard_map/all_to_all | solution.py:41
  59.4 1.9 fusion.123
  63.3 1.8 copy.46
  65.1 19.3 %all-to-all-done.1 = bf16[32,16,1024]{2,1,0:T(8,128)(2,1)S(1)} async-done(((bf16[32,16,1024]{2,1,0:T(8,128)(2,1)}), bf16[32,16,1024]{2,1,0:T(8,128)(2,1)S(1)}, u32[]{:S(2)}, u32[]{:S(2)}) %all-to-all-start.1) | async-done | bytes 1048608 | tf_op jit(solution)/shard_map/all_to_all | solution.py:41
  86.3 3.3 fusion.126
  90.7 2.2 convolution_convert_fusion.2
  93.8 7.6 %collective-permute-done.3.refs_2_ = bf16[512,1792]{1,0:T(8,128)(2,1)S(1)} collective-permute-done((bf16[512,1792]{1,0:T(8,128)(2,1)}, bf16[512,1792]{1,0:T(8,128)(2,1)S(1)}, u32[]{:S(2)}, u32[]{:S(2)}) %collective-permute-start.3) | collective-permute-done | bytes 1835040 | tf_op jit(solution)/shard_map/ppermute | solution.py:33
  101.4 3.4 fusion.12
  105.2 2.7 fusion.18
  107.9 1.8 collective-permute-start.8
  109.7 2.7 fusion.15
  112.4 2.7 fusion.21
  115.1 3.2 collective-permute-done.6
  118.4 3.0 collective-permute-start.7
  121.4 4.3 %collective-permute-done.8 = bf16[128,1792]{1,0:T(8,128)(2,1)S(1)} collective-permute-done((bf16[128,1792]{1,0:T(8,128)(2,1)S(1)}, bf16[128,1792]{1,0:T(8,128)(2,1)S(1)}, u32[]{:S(2)}, u32[]{:S(2)}) %collective-permute-start.8) | collective-permute-done | bytes 458784 | tf_op jit(solution)/shard_map/ppermute | solution.py:33
  125.9 2.7 collective-permute-start.9
  129.0 9.0 %collective-permute-done.9 = bf16[128,1792]{1,0:T(8,128)(2,1)S(1)} collective-permute-done((bf16[128,1792]{1,0:T(8,128)(2,1)S(1)}, bf16[128,1792]{1,0:T(8,128)(2,1)S(1)}, u32[]{:S(2)}, u32[]{:S(2)}) %collective-permute-start.9) | collective-permute-done | bytes 458784 | tf_op jit(solution)/shard_map/ppermute | solution.py:37
  138.2 1.6 multiply_convert_fusion
  140.7 2.1 collective-permute-start.12
  142.8 2.0 fusion.1
  144.8 7.3 %all-to-all-start.2 = ((bf16[32,8,3584]{2,1,0:T(8,128)(2,1)}), bf16[32,8,3584]{2,1,0:T(8,128)(2,1)S(1)}, u32[]{:S(2)}, u32[]{:S(2)}) async-start(bf16[32,8,3584]{2,1,0:T(8,128)(2,1)} %fusion.1), calls=%async_computation.2 | async-start | bytes 3670016 | tf_op jit(solution)/shard_map/all_to_all | solution.py:41
  152.5 11.4 %collective-permute-done.11 = bf16[128,3584]{1,0:T(8,128)(2,1)} collective-permute-done((bf16[128,3584]{1,0:T(8,128)(2,1)S(1)}, bf16[128,3584]{1,0:T(8,128)(2,1)}, u32[]{:S(2)}, u32[]{:S(2)}) %collective-permute-start.11) | collective-permute-done | bytes 917536 | tf_op jit(solution)/shard_map/ppermute | solution.py:33
  163.9 1.5 fusion.34
  165.4 1.6 fusion.27
  167.0 4.0 %convolution_convert_fusion = bf16[768,3584]{1,0:T(8,128)(2,1)} fusion(bf16[128,3584]{1,0:T(8,128)(2,1)S(1)} %get-tuple-element.100, bf16[128,3584]{1,0:T(8,128)(2,1)S(1)} %get-tuple-element.99, pred[768,128]{1,0:T(8,128)(4,1)S(1)} %bitcast.123, pred[768,128]{1,0:T(8,128)(4,1)S(1)} %bitcast.122), kind=kOutput, calls=%fused_computation.2 | convolution fusion | flops 1415905280 | bytes 7536640 | tf_op jit(solution)/shard_map/dot_general | solution.py:25
  170.9 4.2 %collective-permute-done.12 = bf16[192,1792]{1,0:T(8,128)(2,1)} collective-permute-done((bf16[192,1792]{1,0:T(8,128)(2,1)}, bf16[192,1792]{1,0:T(8,128)(2,1)}, u32[]{:S(2)}, u32[]{:S(2)}) %collective-permute-start.12) | collective-permute-done | bytes 688160 | tf_op jit(solution)/shard_map/ppermute | solution.py:33
  175.1 3.0 all-to-all-done.2
  179.4 5.1 %all-to-all-start.3 = ((bf16[32,24,3584]{2,1,0:T(8,128)(2,1)}), bf16[32,24,3584]{2,1,0:T(8,128)(2,1)}, u32[]{:S(2)}, u32[]{:S(2)}) async-start(bf16[32,24,3584]{2,1,0:T(8,128)(2,1)} %bitcast.110), calls=%async_computation.3 | async-start | bytes 11010048 | tf_op jit(solution)/shard_map/all_to_all | solution.py:41
  186.0 3.1 copy-done.2
  189.1 3.1 copy-done.4
  192.2 1.5 copy-done.12
  193.7 3.1 shard_map.118
  196.7 30.1 %collective-permute-done.13.x_ref = bf16[256,3584]{1,0:T(8,128)(2,1)S(1)} collective-permute-done((bf16[256,3584]{1,0:T(8,128)(2,1)}, bf16[256,3584]{1,0:T(8,128)(2,1)S(1)}, u32[]{:S(2)}, u32[]{:S(2)}) %collective-permute-start.13) | collective-permute-done | bytes 1835040 | tf_op jit(solution)/shard_map/ppermute | solution.py:33
  226.8 3.2 copy-done.5
  230.1 3.3 shard_map.119.mine_ref
  233.8 1.3 constant_dynamic-update-slice_fusion.2.refs_3_
  235.1 6.0 %collective-permute-done.14.theirs_ref = bf16[256,512]{1,0:T(8,128)(2,1)S(1)} collective-permute-done((bf16[256,512]{1,0:T(8,128)(2,1)S(1)}, bf16[256,512]{1,0:T(8,128)(2,1)S(1)}, u32[]{:S(2)}, u32[]{:S(2)}) %collective-permute-start.14) | collective-permute-done | bytes 262176 | tf_op jit(solution)/shard_map/ppermute | solution.py:33
  241.1 4.6 %shard_map.120 = bf16[512,1792]{1,0:T(8,128)(2,1)S(1)} custom-call(s32[4]{0:T(128)S(1)} %pad_add_fusion.4.order_ref, bf16[256,512]{1,0:T(8,128)(2,1)S(1)} %shard_map.119.mine_ref, bf16[256,512]{1,0:T(8,128)(2,1)S(1)} %collective-permute-done.14.theirs_ref, bf16[256,256]{1,0:T(8,128)(2,1)S(1)} %fusion.58.place_ref, bf16[1,512,7168]{2,1,0:T(8,128)(2,1)S(1)} %bitcast.102, ...), custom_call_target="tpu_custom_call" | custom-call | flops 1000 | bytes 1000 | tf_op jit(solution)/shard_map/pallas_call | solution.py:129
  248.1 4.7 %all-to-all-done.3 = bf16[32,24,3584]{2,1,0:T(8,128)(2,1)} async-done(((bf16[32,24,3584]{2,1,0:T(8,128)(2,1)}), bf16[32,24,3584]{2,1,0:T(8,128)(2,1)}, u32[]{:S(2)}, u32[]{:S(2)}) %all-to-all-start.3) | async-done | bytes 5505056 | tf_op jit(solution)/shard_map/all_to_all | solution.py:41
  252.8 9.1 %all-to-all-start.4 = ((bf16[32,16,1792]{2,1,0:T(8,128)(2,1)}), bf16[32,16,1792]{2,1,0:T(8,128)(2,1)}, u32[]{:S(2)}, u32[]{:S(2)}) async-start(bf16[32,16,1792]{2,1,0:T(8,128)(2,1)} %bitcast.105), calls=%async_computation.4 | async-start | bytes 3670016 | tf_op jit(solution)/shard_map/all_to_all | solution.py:41
  262.1 3.1 copy-done.3
  265.2 12.1 %shard_map.121.mine_ref = bf16[384,512]{1,0:T(8,128)(2,1)S(1)} custom-call(s32[4]{0:T(128)S(1)} %pad_add_fusion.4.order_ref, bf16[768,3584]{1,0:T(8,128)(2,1)} %bitcast.31.x_ref, bf16[192,192]{1,0:T(8,128)(2,1)S(1)} %get-tuple-element.98.pick_ref, bf16[1,7168,512]{2,1,0:T(8,128)(2,1)S(1)} %copy-done.3, bf16[1,7168,512]{2,1,0:T(8,128)(2,1)} %wu_ref.5), custom_call_target="tpu_custom_call" | custom-call | flops 1000 | bytes 1000 | tf_op jit(solution)/shard_map/pallas_call | solution.py:129
  277.7 11.2 %collective-permute-done.15.theirs_ref = bf16[384,512]{1,0:T(8,128)(2,1)S(1)} collective-permute-done((bf16[384,512]{1,0:T(8,128)(2,1)S(1)}, bf16[384,512]{1,0:T(8,128)(2,1)S(1)}, u32[]{:S(2)}, u32[]{:S(2)}) %collective-permute-start.15) | collective-permute-done | bytes 393248 | tf_op jit(solution)/shard_map/ppermute | solution.py:33
  288.9 7.7 %shard_map.122 = bf16[768,1792]{1,0:T(8,128)(2,1)} custom-call(s32[4]{0:T(128)S(1)} %pad_add_fusion.4.order_ref, bf16[384,512]{1,0:T(8,128)(2,1)S(1)} %shard_map.121.mine_ref, bf16[384,512]{1,0:T(8,128)(2,1)S(1)} %collective-permute-done.15.theirs_ref, bf16[192,192]{1,0:T(8,128)(2,1)S(1)} %get-tuple-element.97.place_ref, bf16[1,512,7168]{2,1,0:T(8,128)(2,1)} %refs_1_.3, ...), custom_call_target="tpu_custom_call" | custom-call | flops 1000 | bytes 1000 | tf_op jit(solution)/shard_map/pallas_call | solution.py:129
  296.6 7.4 %all-to-all-start.5 = ((bf16[32,24,1792]{2,1,0:T(8,128)(2,1)}), bf16[32,24,1792]{2,1,0:T(8,128)(2,1)S(1)}, u32[]{:S(2)}, u32[]{:S(2)}) async-start(bf16[32,24,1792]{2,1,0:T(8,128)(2,1)} %bitcast.34), calls=%async_computation.5 | async-start | bytes 5505024 | tf_op jit(solution)/shard_map/all_to_all | solution.py:41
  304.4 3.0 fusion.131
  307.4 2.9 convolution_add_fusion.2
  310.3 29.7 %all-to-all-done.5 = bf16[32,24,1792]{2,1,0:T(8,128)(2,1)S(1)} async-done(((bf16[32,24,1792]{2,1,0:T(8,128)(2,1)}), bf16[32,24,1792]{2,1,0:T(8,128)(2,1)S(1)}, u32[]{:S(2)}, u32[]{:S(2)}) %all-to-all-start.5) | async-done | bytes 2752544 | tf_op jit(solution)/shard_map/all_to_all | solution.py:41
  340.0 1.8 fusion.11
  341.8 2.6 collective-permute-start.16
  344.5 10.6 %collective-permute-done.16 = bf16[128,1792]{1,0:T(8,128)(2,1)S(1)} collective-permute-done((bf16[128,1792]{1,0:T(8,128)(2,1)S(1)}, bf16[128,1792]{1,0:T(8,128)(2,1)S(1)}, u32[]{:S(2)}, u32[]{:S(2)}) %collective-permute-start.16) | collective-permute-done | bytes 458784 | tf_op jit(solution)/shard_map/ppermute | solution.py:37
  355.1 1.3 add_convert_fusion
  (158 shorter events, 25.9 us)
Async XLA Ops:
  6.5 79.8 %copy-start = (bf16[128,1024]{1,0:T(8,128)(2,1)S(1)}, bf16[128,1024]{1,0:T(8,128)(2,1)}, u32[]{:S(2)}) copy-start(bf16[128,1024]{1,0:T(8,128)(2,1)} %param.12) | copy-start | bytes 786436
  6.5 20.5 %copy-start.27 = (s32[32,3]{0,1:T(4,128)S(1)}, s32[32,3]{0,1:T(4,128)}, u32[]{:S(2)}) copy-start(s32[32,3]{0,1:T(4,128)} %param.15) | copy-start | bytes 1156
  6.5 24.0 %copy-start.26 = (s32[128,8]{0,1:T(8,128)S(1)}, s32[128,8]{0,1:T(8,128)}, u32[]{:S(2)}) copy-start(s32[128,8]{0,1:T(8,128)} %param.22) | copy-start | bytes 12292
  6.5 94.9 %all-gather.2.cloned.1.call-start = ((), (), s32[]{:S(2)}) async-start(), calls=%async_computation.6 | async-start | bytes 15138816 | tf_op jit(solution)/shard_map/all_gather | solution.py:362
  9.2 28.1 %collective-permute-start.1 = (bf16[1,1792]{1,0:T(2,128)(2,1)S(1)}, bf16[1,1792]{1,0:T(2,128)(2,1)S(1)}, u32[]{:S(2)}, u32[]{:S(2)}) collective-permute-start(bf16[1,1792]{1,0:T(2,128)(2,1)S(1)} %broadcast_in_dim.131), channel_id=1, source_target_pairs={{0,3},{1,2},{2,1},{3,0},{4,7},{5,6},{6,5},{7,4},{8,11},{9,10},{10,... | collective-permute-start | bytes 10760 | tf_op jit(solution)/shard_map/ppermute | solution.py:37
  16.7 42.8 %collective-permute-start = (bf16[256,1024]{1,0:T(8,128)(2,1)}, bf16[256,1024]{1,0:T(8,128)(2,1)}, u32[]{:S(2)}, u32[]{:S(2)}) collective-permute-start(bf16[256,1024]{1,0:T(8,128)(2,1)} %constant_dynamic-update-slice_fusion), channel_id=1, source_target_pairs={{0,4},{4,8},{8,12},{12,16},{16,20},{20,24},{24,28},{28,32},{32,36}... | collective-permute-start | bytes 1572872 | tf_op jit(solution)/shard_map/ppermute | solution.py:50
  18.9 26.9 %all-to-all-start = ((bf16[32,8,1024]{2,1,0:T(8,128)(2,1)}), bf16[32,8,1024]{2,1,0:T(8,128)(2,1)S(1)}, u32[]{:S(2)}, u32[]{:S(2)}) async-start(bf16[32,8,1024]{2,1,0:T(8,128)(2,1)} %bitcast.13), calls=%async_computation | async-start | bytes 1048576 | tf_op jit(solution)/shard_map/all_to_all | solution.py:41
  26.9 30.3 %collective-permute-start.5 = (bf16[128,1792]{1,0:T(8,128)(2,1)}, bf16[128,1792]{1,0:T(8,128)(2,1)}, u32[]{:S(2)}, u32[]{:S(2)}) collective-permute-start(bf16[128,1792]{1,0:T(8,128)(2,1)} %param.16), channel_id=1, source_target_pairs={{0,3},{1,2},{2,1},{3,0},{4,7},{5,6},{6,5},{7,4},{8,11},{9,10},{10,... | collective-permute-start | bytes 1376264 | tf_op jit(solution)/shard_map/ppermute | solution.py:37
  28.0 2.7 copy-start.30
  30.9 4.2 %copy-start.17 = (bf16[128,1024]{1,0:T(8,128)(2,1)S(1)}, bf16[128,1024]{1,0:T(8,128)(2,1)}, u32[]{:S(2)}) copy-start(bf16[128,1024]{1,0:T(8,128)(2,1)} %param.13) | copy-start | bytes 786436
  30.9 4.4 %copy-start.18 = (bf16[128,1024]{1,0:T(8,128)(2,1)S(1)}, bf16[128,1024]{1,0:T(8,128)(2,1)}, u32[]{:S(2)}) copy-start(bf16[128,1024]{1,0:T(8,128)(2,1)} %param.14) | copy-start | bytes 786436
  31.0 6.3 %copy-start.25 = (bf16[1792]{0:T(1024)(128)(2,1)S(1)}, bf16[1792]{0:T(1024)(128)(2,1)}, u32[]{:S(2)}) copy-start(bf16[1792]{0:T(1024)(128)(2,1)} %param.18) | copy-start | bytes 10756
  37.4 3.8 %collective-permute-start.2 = (bf16[1,3584]{1,0:T(2,128)(2,1)S(1)}, bf16[1,3584]{1,0:T(2,128)(2,1)S(1)}, u32[]{:S(2)}, u32[]{:S(2)}) collective-permute-start(bf16[1,3584]{1,0:T(2,128)(2,1)S(1)} %pad_maximum_fusion.1.gain_ref), channel_id=1, source_target_pairs={{0,1},{1,0},{2,3},{3,2},{4,5},{5,4},{6,7},{7,6},{8,9},{9,8},{10,11... | collective-permute-start | bytes 21512 | tf_op jit(solution)/shard_map/ppermute | solution.py:33
  43.8 50.0 %collective-permute-start.4 = (bf16[208,1792]{1,0:T(8,128)(2,1)}, bf16[208,1792]{1,0:T(8,128)(2,1)}, u32[]{:S(2)}, u32[]{:S(2)}) collective-permute-start(bf16[208,1792]{1,0:T(8,128)(2,1)} %slice.56), channel_id=1, source_target_pairs={{0,1},{1,0},{2,3},{3,2},{4,5},{5,4},{6,7},{7,6},{8,9},{9,8},{10,11... | collective-permute-start | bytes 2236424 | tf_op jit(solution)/shard_map/ppermute | solution.py:33
  43.8 57.6 %collective-permute-start.3 = (bf16[512,1792]{1,0:T(8,128)(2,1)}, bf16[512,1792]{1,0:T(8,128)(2,1)S(1)}, u32[]{:S(2)}, u32[]{:S(2)}) collective-permute-start(bf16[512,1792]{1,0:T(8,128)(2,1)} %get-tuple-element.40), channel_id=1, source_target_pairs={{0,1},{1,0},{2,3},{3,2},{4,5},{5,4},{6,7},{7,6},{8,9},{9,8},{10,11... | collective-permute-start | bytes 5505032 | tf_op jit(solution)/shard_map/ppermute | solution.py:33
  49.8 34.6 %all-to-all-start.1 = ((bf16[32,16,1024]{2,1,0:T(8,128)(2,1)}), bf16[32,16,1024]{2,1,0:T(8,128)(2,1)S(1)}, u32[]{:S(2)}, u32[]{:S(2)}) async-start(bf16[32,16,1024]{2,1,0:T(8,128)(2,1)} %bitcast_select_fusion.2), calls=%async_computation.1 | async-start | bytes 2097152 | tf_op jit(solution)/shard_map/all_to_all | solution.py:41
  65.1 21.2 %copy-start.23 = (bf16[128,8,128]{2,0,1:T(8,128)(2,1)S(1)}, bf16[128,8,128]{2,0,1:T(8,128)(2,1)}, u32[]{:S(2)}) copy-start(bf16[128,8,128]{2,0,1:T(8,128)(2,1)} %copy.53) | copy-start | bytes 786436
  86.3 3.3 copy-start.16
  89.6 0.9 copy-start.22
  89.6 1.0 copy-start.24
  90.7 2.2 copy-start.28
  101.4 3.4 copy-start.8
  104.8 13.5 %collective-permute-start.6 = (bf16[128,1792]{1,0:T(8,128)(2,1)S(1)}, bf16[128,1792]{1,0:T(8,128)(2,1)S(1)}, u32[]{:S(2)}, u32[]{:S(2)}) collective-permute-start(bf16[128,1792]{1,0:T(8,128)(2,1)S(1)} %fusion.12), channel_id=1, source_target_pairs={{0,1},{1,0},{2,3},{3,2},{4,5},{5,4},{6,7},{7,6},{8,9},{9,8},{10,11... | collective-permute-start | bytes 1376264 | tf_op jit(solution)/shard_map/ppermute | solution.py:33
  107.9 17.9 %collective-permute-start.8 = (bf16[128,1792]{1,0:T(8,128)(2,1)S(1)}, bf16[128,1792]{1,0:T(8,128)(2,1)S(1)}, u32[]{:S(2)}, u32[]{:S(2)}) collective-permute-start(bf16[128,1792]{1,0:T(8,128)(2,1)S(1)} %fusion.18), channel_id=1, source_target_pairs={{0,1},{1,0},{2,3},{3,2},{4,5},{5,4},{6,7},{7,6},{8,9},{9,8},{10,11... | collective-permute-start | bytes 1376264 | tf_op jit(solution)/shard_map/ppermute | solution.py:33
  115.1 13.5 %copy-start.19 = (bf16[112,1792]{1,0:T(8,128)(2,1)S(1)}, bf16[112,1792]{1,0:T(8,128)(2,1)}, u32[]{:S(2)}) copy-start(bf16[112,1792]{1,0:T(8,128)(2,1)} %slice.57) | copy-start | bytes 1204228
  118.4 10.5 %collective-permute-start.7 = (bf16[128,1792]{1,0:T(8,128)(2,1)S(1)}, bf16[128,1792]{1,0:T(8,128)(2,1)S(1)}, u32[]{:S(2)}, u32[]{:S(2)}) collective-permute-start(bf16[128,1792]{1,0:T(8,128)(2,1)S(1)} %add_convert_fusion.2), channel_id=1, source_target_pairs={{0,3},{1,2},{2,1},{3,0},{4,7},{5,6},{6,5},{7,4},{8,11},{9,10},{10,... | collective-permute-start | bytes 1376264 | tf_op jit(solution)/shard_map/ppermute | solution.py:37
  125.8 12.3 %copy-start.15 = (bf16[128,3584]{1,0:T(8,128)(2,1)S(1)}, bf16[128,3584]{1,0:T(8,128)(2,1)}, u32[]{:S(2)}) copy-start(bf16[128,3584]{1,0:T(8,128)(2,1)} %pad_maximum_fusion) | copy-start | bytes 2752516
  125.9 12.2 %collective-permute-start.9 = (bf16[128,1792]{1,0:T(8,128)(2,1)S(1)}, bf16[128,1792]{1,0:T(8,128)(2,1)S(1)}, u32[]{:S(2)}, u32[]{:S(2)}) collective-permute-start(bf16[128,1792]{1,0:T(8,128)(2,1)S(1)} %add_convert_fusion.1), channel_id=1, source_target_pairs={{0,3},{1,2},{2,1},{3,0},{4,7},{5,6},{6,5},{7,4},{8,11},{9,10},{10,... | collective-permute-start | bytes 1376264 | tf_op jit(solution)/shard_map/ppermute | solution.py:37
  128.5 11.2 %collective-permute-start.10 = (bf16[112,1792]{1,0:T(8,128)(2,1)S(1)}, bf16[112,1792]{1,0:T(8,128)(2,1)S(1)}, u32[]{:S(2)}, u32[]{:S(2)}) collective-permute-start(bf16[112,1792]{1,0:T(8,128)(2,1)S(1)} %copy-done.19), channel_id=1, source_target_pairs={{0,1},{1,0},{2,3},{3,2},{4,5},{5,4},{6,7},{7,6},{8,9},{9,8},{10,11... | collective-permute-start | bytes 1204232 | tf_op jit(solution)/shard_map/ppermute | solution.py:33
  138.1 2.3 copy-start.32
  139.7 0.7 copy-start.20
  140.5 23.4 %collective-permute-start.11 = (bf16[128,3584]{1,0:T(8,128)(2,1)S(1)}, bf16[128,3584]{1,0:T(8,128)(2,1)}, u32[]{:S(2)}, u32[]{:S(2)}) collective-permute-start(bf16[128,3584]{1,0:T(8,128)(2,1)S(1)} %get-tuple-element.52), channel_id=1, source_target_pairs={{0,1},{1,0},{2,3},{3,2},{4,5},{5,4},{6,7},{7,6},{8,9},{9,8},{10,11... | collective-permute-start | bytes 2752520 | tf_op jit(solution)/shard_map/ppermute | solution.py:33
  140.7 34.4 %collective-permute-start.12 = (bf16[192,1792]{1,0:T(8,128)(2,1)}, bf16[192,1792]{1,0:T(8,128)(2,1)}, u32[]{:S(2)}, u32[]{:S(2)}) collective-permute-start(bf16[192,1792]{1,0:T(8,128)(2,1)} %slice.58), channel_id=1, source_target_pairs={{0,1},{1,0},{2,3},{3,2},{4,5},{5,4},{6,7},{7,6},{8,9},{9,8},{10,11... | collective-permute-start | bytes 2064392 | tf_op jit(solution)/shard_map/ppermute | solution.py:33
  144.8 33.3 %all-to-all-start.2 = ((bf16[32,8,3584]{2,1,0:T(8,128)(2,1)}), bf16[32,8,3584]{2,1,0:T(8,128)(2,1)S(1)}, u32[]{:S(2)}, u32[]{:S(2)}) async-start(bf16[32,8,3584]{2,1,0:T(8,128)(2,1)} %fusion.1), calls=%async_computation.2 | async-start | bytes 3670016 | tf_op jit(solution)/shard_map/all_to_all | solution.py:41
  178.1 1.2 copy-start.11
  179.4 47.5 %slice-start.2 = ((s8[7340032]{0:T(1024)(128)(4,1)}), s8[3145728]{0:T(1024)(128)(4,1)S(1)}, s32[]{:S(2)}) async-start(s8[7340032]{0:T(1024)(128)(4,1)} %bitcast.103), calls=%async_computation.9 | async-start | bytes 6291456
  179.4 73.5 %all-to-all-start.3 = ((bf16[32,24,3584]{2,1,0:T(8,128)(2,1)}), bf16[32,24,3584]{2,1,0:T(8,128)(2,1)}, u32[]{:S(2)}, u32[]{:S(2)}) async-start(bf16[32,24,3584]{2,1,0:T(8,128)(2,1)} %bitcast.110), calls=%async_computation.3 | async-start | bytes 11010048 | tf_op jit(solution)/shard_map/all_to_all | solution.py:41
  184.5 42.3 %collective-permute-start.13 = (bf16[256,3584]{1,0:T(8,128)(2,1)}, bf16[256,3584]{1,0:T(8,128)(2,1)S(1)}, u32[]{:S(2)}, u32[]{:S(2)}) collective-permute-start(bf16[256,3584]{1,0:T(8,128)(2,1)} %bitcast.106), channel_id=1, source_target_pairs={{0,1},{1,0},{2,3},{3,2},{4,5},{5,4},{6,7},{7,6},{8,9},{9,8},{10,11... | collective-permute-start | bytes 5505032 | tf_op jit(solution)/shard_map/ppermute | solution.py:33
  186.0 3.1 copy-start.2
  189.1 3.1 copy-start.4
  192.2 1.5 copy-start.12
  193.7 33.2 %slice-start.3 = ((s8[7340032]{0:T(1024)(128)(4,1)}), s8[4194304]{0:T(1024)(128)(4,1)S(1)}, s32[]{:S(2)}) async-start(s8[7340032]{0:T(1024)(128)(4,1)} %bitcast.103), calls=%async_computation.10 | async-start | bytes 8388608
  226.8 14.2 %slice-start = ((s8[7340032]{0:T(1024)(128)(4,1)}), s8[4194304]{0:T(1024)(128)(4,1)S(1)}, s32[]{:S(2)}) async-start(s8[7340032]{0:T(1024)(128)(4,1)} %bitcast.101), calls=%async_computation.7 | async-start | bytes 8388608
  226.8 3.2 copy-start.5
  230.1 3.7 %copy-start.21 = (bf16[112,1792]{1,0:T(8,128)(2,1)S(1)}, bf16[112,1792]{1,0:T(8,128)(2,1)}, u32[]{:S(2)}) copy-start(bf16[112,1792]{1,0:T(8,128)(2,1)} %copy-done.20) | copy-start | bytes 1204228
  230.1 11.0 %slice-start.1 = ((s8[7340032]{0:T(1024)(128)(4,1)}), s8[3145728]{0:T(1024)(128)(4,1)S(1)}, s32[]{:S(2)}) async-start(s8[7340032]{0:T(1024)(128)(4,1)} %bitcast.101), calls=%async_computation.8 | async-start | bytes 6291456
  233.4 7.7 %copy-start.9 = (bf16[512,1792]{1,0:T(8,128)(2,1)S(1)}, bf16[512,1792]{1,0:T(8,128)(2,1)}, u32[]{:S(2)}) copy-start(bf16[512,1792]{1,0:T(8,128)(2,1)} %copy-done.8) | copy-start | bytes 5505028
  233.4 7.7 %collective-permute-start.14 = (bf16[256,512]{1,0:T(8,128)(2,1)S(1)}, bf16[256,512]{1,0:T(8,128)(2,1)S(1)}, u32[]{:S(2)}, u32[]{:S(2)}) collective-permute-start(bf16[256,512]{1,0:T(8,128)(2,1)S(1)} %shard_map.119.mine_ref), channel_id=1, source_target_pairs={{0,1},{1,0},{2,3},{3,2},{4,5},{5,4},{6,7},{7,6},{8,9},{9,8},{10,11... | collective-permute-start | bytes 786440 | tf_op jit(solution)/shard_map/ppermute | solution.py:33
  245.7 1.2 copy-start.6
  246.9 1.2 copy-start.10
  252.8 43.7 %all-to-all-start.4 = ((bf16[32,16,1792]{2,1,0:T(8,128)(2,1)}), bf16[32,16,1792]{2,1,0:T(8,128)(2,1)}, u32[]{:S(2)}, u32[]{:S(2)}) async-start(bf16[32,16,1792]{2,1,0:T(8,128)(2,1)} %bitcast.105), calls=%async_computation.4 | async-start | bytes 3670016 | tf_op jit(solution)/shard_map/all_to_all | solution.py:41
  262.1 3.1 copy-start.3
  265.2 23.7 %copy-start.7 = (bf16[512,1792]{1,0:T(8,128)(2,1)S(1)}, bf16[512,1792]{1,0:T(8,128)(2,1)}, u32[]{:S(2)}) copy-start(bf16[512,1792]{1,0:T(8,128)(2,1)} %copy-done.6) | copy-start | bytes 5505028
  277.3 11.5 %collective-permute-start.15 = (bf16[384,512]{1,0:T(8,128)(2,1)S(1)}, bf16[384,512]{1,0:T(8,128)(2,1)S(1)}, u32[]{:S(2)}, u32[]{:S(2)}) collective-permute-start(bf16[384,512]{1,0:T(8,128)(2,1)S(1)} %shard_map.121.mine_ref), channel_id=1, source_target_pairs={{0,1},{1,0},{2,3},{3,2},{4,5},{5,4},{6,7},{7,6},{8,9},{9,8},{10,11... | collective-permute-start | bytes 1179656 | tf_op jit(solution)/shard_map/ppermute | solution.py:33
  296.5 7.4 %copy-start.29 = (bf16[128,8]{0,1:T(8,128)(2,1)S(1)}, bf16[128,8]{0,1:T(8,128)(2,1)}, u32[]{:S(2)}) copy-start(bf16[128,8]{0,1:T(8,128)(2,1)} %param.23) | copy-start | bytes 6148
  296.5 7.5 %copy-start.31 = (s32[32]{0:T(128)S(1)}, s32[32]{0:T(128)}, u32[]{:S(2)}) copy-start(s32[32]{0:T(128)} %copy-done.30) | copy-start | bytes 388
  296.6 43.4 %all-to-all-start.5 = ((bf16[32,24,1792]{2,1,0:T(8,128)(2,1)}), bf16[32,24,1792]{2,1,0:T(8,128)(2,1)S(1)}, u32[]{:S(2)}, u32[]{:S(2)}) async-start(bf16[32,24,1792]{2,1,0:T(8,128)(2,1)} %bitcast.34), calls=%async_computation.5 | async-start | bytes 5505024 | tf_op jit(solution)/shard_map/all_to_all | solution.py:41
  304.0 3.4 copy-start.13
  340.0 15.1 %copy-start.14 = (f32[128,1792]{1,0:T(8,128)S(1)}, f32[128,1792]{1,0:T(8,128)}, u32[]{:S(2)}) copy-start(f32[128,1792]{1,0:T(8,128)} %convolution_add_fusion.2) | copy-start | bytes 2752516
  340.0 16.4 %copy-start.1 = (bf16[128,1024]{1,0:T(8,128)(2,1)S(1)}, bf16[128,1024]{1,0:T(8,128)(2,1)}, u32[]{:S(2)}) copy-start(bf16[128,1024]{1,0:T(8,128)(2,1)} %param.12) | copy-start | bytes 786436
  341.8 13.3 %collective-permute-start.16 = (bf16[128,1792]{1,0:T(8,128)(2,1)S(1)}, bf16[128,1792]{1,0:T(8,128)(2,1)S(1)}, u32[]{:S(2)}, u32[]{:S(2)}) collective-permute-start(bf16[128,1792]{1,0:T(8,128)(2,1)S(1)} %fusion.11), channel_id=1, source_target_pairs={{0,3},{1,2},{2,1},{3,0},{4,7},{5,6},{6,5},{7,4},{8,11},{9,10},{10,... | collective-permute-start | bytes 1376264 | tf_op jit(solution)/shard_map/ppermute | solution.py:37
Sparse Core Ops, SparseCore 0:
  9.6 85.4 all-gather.1

commit v2 on v1

--- a/solution.py
+++ b/solution.py
@@ -409,10 +409,10 @@
     attended = attend(query_states, key_states, value_states, selected, heads)
     attended = regroup(attended, heads, count)
     late = [down_given[1][EARLY:MIDDLE], down_given[1][MIDDLE:]]
-    attended, early, late, residual_half = lax.optimization_barrier(
-        (attended, early, late, residual_half)
-    )
-    total, late = project_sum(attended, full_out, order, theirs_order, width, late)
+    attended, late, residual_half = lax.optimization_barrier((attended, late, residual_half))
+    total, (late, early) = project_sum(
+        attended, full_out, order, theirs_order, width, (late, early)
+    )
     late = [half_swap(block) for block in late]
     hidden = (total + residual_half.astype(F32)).astype(BF16).astype(F32)
     gained = (hidden * gain_mine.astype(F32)).astype(BF16)

time: 365 us -> 360 us (0.986)
    unnamed x81 -> x77, local copies, waits for them, and re-layouts: 23.2 us -> 22.6 us
  transfers between devices with their start and end apart: 24 -> 24, of which waited for: 16 -> 16; matrix products, arithmetic and copies ran while one was open for 18% -> 19% of each run, Pallas kernels for 8% -> 9%
where the time goes in v2:
time: 360 us; the launch traced here: 359 us
  waiting for transfers between devices  157 us (44%)
  starting transfers between devices  65.2 us (18%)
  local copies, waits for them, and re-layouts  44.9 us (12%)
  matrix products  32.2 us (9%)
  Pallas kernels  30.7 us (9%)
  other arithmetic  14.7 us (4%)
  between operations  14.1 us (4%)
    ppermute x11, waiting for transfers between devices, half_swap(): return lax.ppermute(block, 'exp', [(i, i ^ 1) for i in range(4)])  78.5 us
    all_to_all x6, waiting for transfers between devices, spread(): return lax.all_to_all(block, 'seq', split_axis=0, concat_axis=0, tiled=True)  54.5 us
    all_to_all x6, starting transfers between devices, spread(): return lax.all_to_all(block, 'seq', split_axis=0, concat_axis=0, tiled=True)  43.3 us
    pallas_call x5, Pallas kernels, call(): pl.pallas_call(kernel, grid_spec=pltpu.PrefetchScalarGridSpec(num_scalar_...  30.7 us
    unnamed x77, local copies, waits for them, and re-layouts  22.6 us
    ppermute x5, waiting for transfers between devices, group_swap(): return lax.ppermute(block, 'exp', [(i, 3 - i) for i in range(4)])  21 us
    dot_general x8, matrix products, dot(): return jnp.dot(a, b, preferred_element_type=F32)  17.8 us
    ppermute x5, starting transfers between devices, group_swap(): return lax.ppermute(block, 'exp', [(i, 3 - i) for i in range(4)])  12.4 us
  transfers between devices with their start and end apart: 24, of which 16 were waited for; matrix products, arithmetic and copies ran while one was open for 19% of the time, Pallas kernels for 9%

profile of v2, /device:TPU:0, one launch (start us, length us, event | category | flops | bytes accessed | tf_op | source)
XLA Modules:
  0.0 358.6 jit_solution(1749528294993522509)
XLA Ops:
  6.5 1.9 reshape.220
  9.2 4.1 %collective-permute-start.1 = (bf16[1,1792]{1,0:T(2,128)(2,1)S(1)}, bf16[1,1792]{1,0:T(2,128)(2,1)S(1)}, u32[]{:S(2)}, u32[]{:S(2)}) collective-permute-start(bf16[1,1792]{1,0:T(2,128)(2,1)S(1)} %broadcast_in_dim.131), channel_id=1, source_target_pairs={{0,3},{1,2},{2,1},{3,0},{4,7},{5,6},{6,5},{7,4},{8,11},{9,10},{10,... | collective-permute-start | bytes 10760 | tf_op jit(solution)/shard_map/ppermute | solution.py:37
  13.3 1.7 constant_dynamic-update-slice_fusion.1
  15.0 1.7 constant_dynamic-update-slice_fusion
  16.7 2.3 collective-permute-start
  18.9 8.0 %all-to-all-start = ((bf16[32,8,1024]{2,1,0:T(8,128)(2,1)}), bf16[32,8,1024]{2,1,0:T(8,128)(2,1)S(1)}, u32[]{:S(2)}, u32[]{:S(2)}) async-start(bf16[32,8,1024]{2,1,0:T(8,128)(2,1)} %bitcast.13), calls=%async_computation | async-start | bytes 1048576 | tf_op jit(solution)/shard_map/all_to_all | solution.py:41
  28.6 1.3 compare_select_fusion.5
  31.0 3.6 %dynamic-slice_bitcast_fusion = (bf16[512,1792]{1,0:T(8,128)(2,1)S(1)}, bf16[512,1792]{1,0:T(8,128)(2,1)}) fusion(bf16[1,512,7168]{2,1,0:T(8,128)(2,1)} %refs_1_.3, s32[]{:T(128)S(6)} %select_n.244, s32[]{:T(128)S(6)} %select_n.243), kind=kLoop, calls=%fused_computation.42 | loop fusion | bytes 7340040 | tf_op jit(solution)/shard_map/dynamic_slice | solution.py:369
  37.5 3.7 %collective-permute-done.2.gain_ref = bf16[1,3584]{1,0:T(2,128)(2,1)S(1)} collective-permute-done((bf16[1,3584]{1,0:T(2,128)(2,1)S(1)}, bf16[1,3584]{1,0:T(2,128)(2,1)S(1)}, u32[]{:S(2)}, u32[]{:S(2)}) %collective-permute-start.2) | collective-permute-done | bytes 7200 | tf_op jit(solution)/shard_map/ppermute | solution.py:33
  43.8 2.0 collective-permute-start.5
  45.8 1.6 gather_fusion
  47.4 2.4 bitcast_select_fusion.2
  49.8 7.4 %all-to-all-start.1 = ((bf16[32,16,1024]{2,1,0:T(8,128)(2,1)}), bf16[32,16,1024]{2,1,0:T(8,128)(2,1)S(1)}, u32[]{:S(2)}, u32[]{:S(2)}) async-start(bf16[32,16,1024]{2,1,0:T(8,128)(2,1)} %bitcast_select_fusion.2), calls=%async_computation.1 | async-start | bytes 2097152 | tf_op jit(solution)/shard_map/all_to_all | solution.py:41
  59.5 1.9 fusion.123
  63.4 1.8 copy.46
  65.2 19.2 %all-to-all-done.1 = bf16[32,16,1024]{2,1,0:T(8,128)(2,1)S(1)} async-done(((bf16[32,16,1024]{2,1,0:T(8,128)(2,1)}), bf16[32,16,1024]{2,1,0:T(8,128)(2,1)S(1)}, u32[]{:S(2)}, u32[]{:S(2)}) %all-to-all-start.1) | async-done | bytes 1048608 | tf_op jit(solution)/shard_map/all_to_all | solution.py:41
  86.0 3.2 fusion.126
  89.2 2.1 convolution_convert_fusion.2
  92.3 2.8 all-gather.2.cloned.1.call-done
  95.1 2.7 fusion.12
  97.8 1.6 collective-permute-start.4
  99.4 2.7 fusion.18
  102.7 2.7 fusion.15
  105.4 2.7 fusion.21
  108.1 3.8 %collective-permute-done.4 = bf16[128,1792]{1,0:T(8,128)(2,1)S(1)} collective-permute-done((bf16[128,1792]{1,0:T(8,128)(2,1)S(1)}, bf16[128,1792]{1,0:T(8,128)(2,1)S(1)}, u32[]{:S(2)}, u32[]{:S(2)}) %collective-permute-start.4) | collective-permute-done | bytes 458784 | tf_op jit(solution)/shard_map/ppermute | solution.py:33
  112.0 2.9 collective-permute-start.7
  114.9 6.1 %collective-permute-done.8 = bf16[128,1792]{1,0:T(8,128)(2,1)S(1)} collective-permute-done((bf16[128,1792]{1,0:T(8,128)(2,1)S(1)}, bf16[128,1792]{1,0:T(8,128)(2,1)S(1)}, u32[]{:S(2)}, u32[]{:S(2)}) %collective-permute-start.8) | collective-permute-done | bytes 458784 | tf_op jit(solution)/shard_map/ppermute | solution.py:33
  121.2 3.0 collective-permute-start.9
  124.7 9.7 %collective-permute-done.9 = bf16[128,1792]{1,0:T(8,128)(2,1)S(1)} collective-permute-done((bf16[128,1792]{1,0:T(8,128)(2,1)S(1)}, bf16[128,1792]{1,0:T(8,128)(2,1)S(1)}, u32[]{:S(2)}, u32[]{:S(2)}) %collective-permute-start.9) | collective-permute-done | bytes 458784 | tf_op jit(solution)/shard_map/ppermute | solution.py:37
  134.5 1.6 multiply_convert_fusion
  137.2 2.1 collective-permute-start.12
  139.3 1.9 fusion.1
  141.2 6.3 %all-to-all-start.2 = ((bf16[32,8,3584]{2,1,0:T(8,128)(2,1)}), bf16[32,8,3584]{2,1,0:T(8,128)(2,1)S(1)}, u32[]{:S(2)}, u32[]{:S(2)}) async-start(bf16[32,8,3584]{2,1,0:T(8,128)(2,1)} %fusion.1), calls=%async_computation.2 | async-start | bytes 3670016 | tf_op jit(solution)/shard_map/all_to_all | solution.py:41
  147.8 12.5 %collective-permute-done.11 = bf16[128,3584]{1,0:T(8,128)(2,1)} collective-permute-done((bf16[128,3584]{1,0:T(8,128)(2,1)S(1)}, bf16[128,3584]{1,0:T(8,128)(2,1)}, u32[]{:S(2)}, u32[]{:S(2)}) %collective-permute-start.11) | collective-permute-done | bytes 917536 | tf_op jit(solution)/shard_map/ppermute | solution.py:33
  160.3 1.5 fusion.34
  161.8 1.6 fusion.27
  163.4 4.0 %convolution_convert_fusion = bf16[768,3584]{1,0:T(8,128)(2,1)} fusion(bf16[128,3584]{1,0:T(8,128)(2,1)S(1)} %get-tuple-element.100, bf16[128,3584]{1,0:T(8,128)(2,1)S(1)} %get-tuple-element.99, pred[768,128]{1,0:T(8,128)(4,1)S(1)} %bitcast.123, pred[768,128]{1,0:T(8,128)(4,1)S(1)} %bitcast.122), kind=kOutput, calls=%fused_computation.2 | convolution fusion | flops 1415905280 | bytes 7536640 | tf_op jit(solution)/shard_map/dot_general | solution.py:25
  167.5 5.2 %collective-permute-done.12 = bf16[192,1792]{1,0:T(8,128)(2,1)} collective-permute-done((bf16[192,1792]{1,0:T(8,128)(2,1)}, bf16[192,1792]{1,0:T(8,128)(2,1)}, u32[]{:S(2)}, u32[]{:S(2)}) %collective-permute-start.12) | collective-permute-done | bytes 688160 | tf_op jit(solution)/shard_map/ppermute | solution.py:33
  173.5 1.2 copy-done.11
  174.7 5.2 %all-to-all-start.3 = ((bf16[32,24,3584]{2,1,0:T(8,128)(2,1)}), bf16[32,24,3584]{2,1,0:T(8,128)(2,1)}, u32[]{:S(2)}, u32[]{:S(2)}) async-start(bf16[32,24,3584]{2,1,0:T(8,128)(2,1)} %bitcast.110), calls=%async_computation.3 | async-start | bytes 11010048 | tf_op jit(solution)/shard_map/all_to_all | solution.py:41
  181.4 3.1 copy-done.2
  184.5 3.1 copy-done.4
  187.6 1.5 copy-done.12
  189.1 3.0 shard_map.118
  192.1 30.1 %collective-permute-done.13.x_ref = bf16[256,3584]{1,0:T(8,128)(2,1)S(1)} collective-permute-done((bf16[256,3584]{1,0:T(8,128)(2,1)}, bf16[256,3584]{1,0:T(8,128)(2,1)S(1)}, u32[]{:S(2)}, u32[]{:S(2)}) %collective-permute-start.13) | collective-permute-done | bytes 1835040 | tf_op jit(solution)/shard_map/ppermute | solution.py:33
  222.2 3.2 copy-done.5
  225.5 3.3 shard_map.119.mine_ref
  229.2 1.3 constant_dynamic-update-slice_fusion.2.refs_3_
  230.5 6.0 %collective-permute-done.14.theirs_ref = bf16[256,512]{1,0:T(8,128)(2,1)S(1)} collective-permute-done((bf16[256,512]{1,0:T(8,128)(2,1)S(1)}, bf16[256,512]{1,0:T(8,128)(2,1)S(1)}, u32[]{:S(2)}, u32[]{:S(2)}) %collective-permute-start.14) | collective-permute-done | bytes 262176 | tf_op jit(solution)/shard_map/ppermute | solution.py:33
  236.5 4.6 %shard_map.120 = bf16[512,1792]{1,0:T(8,128)(2,1)S(1)} custom-call(s32[4]{0:T(128)S(1)} %pad_add_fusion.4.order_ref, bf16[256,512]{1,0:T(8,128)(2,1)S(1)} %shard_map.119.mine_ref, bf16[256,512]{1,0:T(8,128)(2,1)S(1)} %collective-permute-done.14.theirs_ref, bf16[256,256]{1,0:T(8,128)(2,1)S(1)} %fusion.58.place_ref, bf16[1,512,7168]{2,1,0:T(8,128)(2,1)S(1)} %bitcast.102, ...), custom_call_target="tpu_custom_call" | custom-call | flops 1000 | bytes 1000 | tf_op jit(solution)/shard_map/pallas_call | solution.py:129
  243.5 4.7 %all-to-all-done.3 = bf16[32,24,3584]{2,1,0:T(8,128)(2,1)} async-done(((bf16[32,24,3584]{2,1,0:T(8,128)(2,1)}), bf16[32,24,3584]{2,1,0:T(8,128)(2,1)}, u32[]{:S(2)}, u32[]{:S(2)}) %all-to-all-start.3) | async-done | bytes 5505056 | tf_op jit(solution)/shard_map/all_to_all | solution.py:41
  248.2 9.1 %all-to-all-start.4 = ((bf16[32,16,1792]{2,1,0:T(8,128)(2,1)}), bf16[32,16,1792]{2,1,0:T(8,128)(2,1)}, u32[]{:S(2)}, u32[]{:S(2)}) async-start(bf16[32,16,1792]{2,1,0:T(8,128)(2,1)} %bitcast.105), calls=%async_computation.4 | async-start | bytes 3670016 | tf_op jit(solution)/shard_map/all_to_all | solution.py:41
  257.5 3.1 copy-done.3
  260.6 12.1 %shard_map.121.mine_ref = bf16[384,512]{1,0:T(8,128)(2,1)S(1)} custom-call(s32[4]{0:T(128)S(1)} %pad_add_fusion.4.order_ref, bf16[768,3584]{1,0:T(8,128)(2,1)} %bitcast.31.x_ref, bf16[192,192]{1,0:T(8,128)(2,1)S(1)} %get-tuple-element.98.pick_ref, bf16[1,7168,512]{2,1,0:T(8,128)(2,1)S(1)} %copy-done.3, bf16[1,7168,512]{2,1,0:T(8,128)(2,1)} %wu_ref.5), custom_call_target="tpu_custom_call" | custom-call | flops 1000 | bytes 1000 | tf_op jit(solution)/shard_map/pallas_call | solution.py:129
  273.0 11.2 %collective-permute-done.15.theirs_ref = bf16[384,512]{1,0:T(8,128)(2,1)S(1)} collective-permute-done((bf16[384,512]{1,0:T(8,128)(2,1)S(1)}, bf16[384,512]{1,0:T(8,128)(2,1)S(1)}, u32[]{:S(2)}, u32[]{:S(2)}) %collective-permute-start.15) | collective-permute-done | bytes 393248 | tf_op jit(solution)/shard_map/ppermute | solution.py:33
  284.3 7.6 %shard_map.122 = bf16[768,1792]{1,0:T(8,128)(2,1)} custom-call(s32[4]{0:T(128)S(1)} %pad_add_fusion.4.order_ref, bf16[384,512]{1,0:T(8,128)(2,1)S(1)} %shard_map.121.mine_ref, bf16[384,512]{1,0:T(8,128)(2,1)S(1)} %collective-permute-done.15.theirs_ref, bf16[192,192]{1,0:T(8,128)(2,1)S(1)} %get-tuple-element.97.place_ref, bf16[1,512,7168]{2,1,0:T(8,128)(2,1)} %refs_1_.3, ...), custom_call_target="tpu_custom_call" | custom-call | flops 1000 | bytes 1000 | tf_op jit(solution)/shard_map/pallas_call | solution.py:129
  291.9 7.4 %all-to-all-start.5 = ((bf16[32,24,1792]{2,1,0:T(8,128)(2,1)}), bf16[32,24,1792]{2,1,0:T(8,128)(2,1)S(1)}, u32[]{:S(2)}, u32[]{:S(2)}) async-start(bf16[32,24,1792]{2,1,0:T(8,128)(2,1)} %bitcast.34), calls=%async_computation.5 | async-start | bytes 5505024 | tf_op jit(solution)/shard_map/all_to_all | solution.py:41
  299.7 3.0 fusion.131
  302.8 2.9 convolution_add_fusion.2
  305.7 29.7 %all-to-all-done.5 = bf16[32,24,1792]{2,1,0:T(8,128)(2,1)S(1)} async-done(((bf16[32,24,1792]{2,1,0:T(8,128)(2,1)}), bf16[32,24,1792]{2,1,0:T(8,128)(2,1)S(1)}, u32[]{:S(2)}, u32[]{:S(2)}) %all-to-all-start.5) | async-done | bytes 2752544 | tf_op jit(solution)/shard_map/all_to_all | solution.py:41
  335.3 1.8 fusion.11
  337.2 2.3 collective-permute-start.16
  339.5 11.0 %collective-permute-done.16 = bf16[128,1792]{1,0:T(8,128)(2,1)S(1)} collective-permute-done((bf16[128,1792]{1,0:T(8,128)(2,1)S(1)}, bf16[128,1792]{1,0:T(8,128)(2,1)S(1)}, u32[]{:S(2)}, u32[]{:S(2)}) %collective-permute-start.16) | collective-permute-done | bytes 458784 | tf_op jit(solution)/shard_map/ppermute | solution.py:37
  350.4 1.3 add_convert_fusion
  (154 shorter events, 24.4 us)
Async XLA Ops:
  6.5 79.4 %copy-start = (bf16[128,1024]{1,0:T(8,128)(2,1)S(1)}, bf16[128,1024]{1,0:T(8,128)(2,1)}, u32[]{:S(2)}) copy-start(bf16[128,1024]{1,0:T(8,128)(2,1)} %param.12) | copy-start | bytes 786436
  6.5 20.5 %copy-start.25 = (s32[32,3]{0,1:T(4,128)S(1)}, s32[32,3]{0,1:T(4,128)}, u32[]{:S(2)}) copy-start(s32[32,3]{0,1:T(4,128)} %param.15) | copy-start | bytes 1156
  6.5 24.0 %copy-start.24 = (s32[128,8]{0,1:T(8,128)S(1)}, s32[128,8]{0,1:T(8,128)}, u32[]{:S(2)}) copy-start(s32[128,8]{0,1:T(8,128)} %param.22) | copy-start | bytes 12292
  6.5 88.5 %all-gather.2.cloned.1.call-start = ((), (), s32[]{:S(2)}) async-start(), calls=%async_computation.6 | async-start | bytes 15138816 | tf_op jit(solution)/shard_map/all_gather | solution.py:362
  9.2 28.0 %collective-permute-start.1 = (bf16[1,1792]{1,0:T(2,128)(2,1)S(1)}, bf16[1,1792]{1,0:T(2,128)(2,1)S(1)}, u32[]{:S(2)}, u32[]{:S(2)}) collective-permute-start(bf16[1,1792]{1,0:T(2,128)(2,1)S(1)} %broadcast_in_dim.131), channel_id=1, source_target_pairs={{0,3},{1,2},{2,1},{3,0},{4,7},{5,6},{6,5},{7,4},{8,11},{9,10},{10,... | collective-permute-start | bytes 10760 | tf_op jit(solution)/shard_map/ppermute | solution.py:37
  16.7 42.8 %collective-permute-start = (bf16[256,1024]{1,0:T(8,128)(2,1)}, bf16[256,1024]{1,0:T(8,128)(2,1)}, u32[]{:S(2)}, u32[]{:S(2)}) collective-permute-start(bf16[256,1024]{1,0:T(8,128)(2,1)} %constant_dynamic-update-slice_fusion), channel_id=1, source_target_pairs={{0,4},{4,8},{8,12},{12,16},{16,20},{20,24},{24,28},{28,32},{32,36}... | collective-permute-start | bytes 1572872 | tf_op jit(solution)/shard_map/ppermute | solution.py:50
  18.9 26.9 %all-to-all-start = ((bf16[32,8,1024]{2,1,0:T(8,128)(2,1)}), bf16[32,8,1024]{2,1,0:T(8,128)(2,1)S(1)}, u32[]{:S(2)}, u32[]{:S(2)}) async-start(bf16[32,8,1024]{2,1,0:T(8,128)(2,1)} %bitcast.13), calls=%async_computation | async-start | bytes 1048576 | tf_op jit(solution)/shard_map/all_to_all | solution.py:41
  26.9 30.3 %collective-permute-start.3 = (bf16[128,1792]{1,0:T(8,128)(2,1)}, bf16[128,1792]{1,0:T(8,128)(2,1)}, u32[]{:S(2)}, u32[]{:S(2)}) collective-permute-start(bf16[128,1792]{1,0:T(8,128)(2,1)} %param.16), channel_id=1, source_target_pairs={{0,3},{1,2},{2,1},{3,0},{4,7},{5,6},{6,5},{7,4},{8,11},{9,10},{10,... | collective-permute-start | bytes 1376264 | tf_op jit(solution)/shard_map/ppermute | solution.py:37
  28.0 2.7 copy-start.28
  31.0 4.2 %copy-start.16 = (bf16[128,1024]{1,0:T(8,128)(2,1)S(1)}, bf16[128,1024]{1,0:T(8,128)(2,1)}, u32[]{:S(2)}) copy-start(bf16[128,1024]{1,0:T(8,128)(2,1)} %param.13) | copy-start | bytes 786436
  31.0 4.4 %copy-start.17 = (bf16[128,1024]{1,0:T(8,128)(2,1)S(1)}, bf16[128,1024]{1,0:T(8,128)(2,1)}, u32[]{:S(2)}) copy-start(bf16[128,1024]{1,0:T(8,128)(2,1)} %param.14) | copy-start | bytes 786436
  31.0 6.2 %copy-start.23 = (bf16[1792]{0:T(1024)(128)(2,1)S(1)}, bf16[1792]{0:T(1024)(128)(2,1)}, u32[]{:S(2)}) copy-start(bf16[1792]{0:T(1024)(128)(2,1)} %param.18) | copy-start | bytes 10756
  37.3 3.8 %collective-permute-start.2 = (bf16[1,3584]{1,0:T(2,128)(2,1)S(1)}, bf16[1,3584]{1,0:T(2,128)(2,1)S(1)}, u32[]{:S(2)}, u32[]{:S(2)}) collective-permute-start(bf16[1,3584]{1,0:T(2,128)(2,1)S(1)} %pad_maximum_fusion.1.gain_ref), channel_id=1, source_target_pairs={{0,1},{1,0},{2,3},{3,2},{4,5},{5,4},{6,7},{7,6},{8,9},{9,8},{10,11... | collective-permute-start | bytes 21512 | tf_op jit(solution)/shard_map/ppermute | solution.py:33
  43.8 68.1 %collective-permute-start.6 = (bf16[208,1792]{1,0:T(8,128)(2,1)}, bf16[208,1792]{1,0:T(8,128)(2,1)}, u32[]{:S(2)}, u32[]{:S(2)}) collective-permute-start(bf16[208,1792]{1,0:T(8,128)(2,1)} %slice.58), channel_id=1, source_target_pairs={{0,1},{1,0},{2,3},{3,2},{4,5},{5,4},{6,7},{7,6},{8,9},{9,8},{10,11... | collective-permute-start | bytes 2236424 | tf_op jit(solution)/shard_map/ppermute | solution.py:33
  43.8 68.1 %collective-permute-start.5 = (bf16[512,1792]{1,0:T(8,128)(2,1)}, bf16[512,1792]{1,0:T(8,128)(2,1)S(1)}, u32[]{:S(2)}, u32[]{:S(2)}) collective-permute-start(bf16[512,1792]{1,0:T(8,128)(2,1)} %get-tuple-element.46), channel_id=1, source_target_pairs={{0,1},{1,0},{2,3},{3,2},{4,5},{5,4},{6,7},{7,6},{8,9},{9,8},{10,11... | collective-permute-start | bytes 5505032 | tf_op jit(solution)/shard_map/ppermute | solution.py:33
  49.8 34.6 %all-to-all-start.1 = ((bf16[32,16,1024]{2,1,0:T(8,128)(2,1)}), bf16[32,16,1024]{2,1,0:T(8,128)(2,1)S(1)}, u32[]{:S(2)}, u32[]{:S(2)}) async-start(bf16[32,16,1024]{2,1,0:T(8,128)(2,1)} %bitcast_select_fusion.2), calls=%async_computation.1 | async-start | bytes 2097152 | tf_op jit(solution)/shard_map/all_to_all | solution.py:41
  86.0 3.2 copy-start.18
  86.0 3.2 copy-start.22
  89.2 2.1 copy-start.26
  97.8 14.1 %collective-permute-start.4 = (bf16[128,1792]{1,0:T(8,128)(2,1)S(1)}, bf16[128,1792]{1,0:T(8,128)(2,1)S(1)}, u32[]{:S(2)}, u32[]{:S(2)}) collective-permute-start(bf16[128,1792]{1,0:T(8,128)(2,1)S(1)} %fusion.12), channel_id=1, source_target_pairs={{0,1},{1,0},{2,3},{3,2},{4,5},{5,4},{6,7},{7,6},{8,9},{9,8},{10,11... | collective-permute-start | bytes 1376264 | tf_op jit(solution)/shard_map/ppermute | solution.py:33
  102.1 18.9 %collective-permute-start.8 = (bf16[128,1792]{1,0:T(8,128)(2,1)S(1)}, bf16[128,1792]{1,0:T(8,128)(2,1)S(1)}, u32[]{:S(2)}, u32[]{:S(2)}) collective-permute-start(bf16[128,1792]{1,0:T(8,128)(2,1)S(1)} %fusion.18), channel_id=1, source_target_pairs={{0,1},{1,0},{2,3},{3,2},{4,5},{5,4},{6,7},{7,6},{8,9},{9,8},{10,11... | collective-permute-start | bytes 1376264 | tf_op jit(solution)/shard_map/ppermute | solution.py:33
  108.1 16.1 %copy-start.19 = (bf16[112,1792]{1,0:T(8,128)(2,1)S(1)}, bf16[112,1792]{1,0:T(8,128)(2,1)}, u32[]{:S(2)}) copy-start(bf16[112,1792]{1,0:T(8,128)(2,1)} %slice.56) | copy-start | bytes 1204228
  111.8 12.9 %copy-start.8 = (bf16[512,1792]{1,0:T(8,128)(2,1)}, bf16[512,1792]{1,0:T(8,128)(2,1)S(1)}, u32[]{:S(2)}) copy-start(bf16[512,1792]{1,0:T(8,128)(2,1)S(1)} %collective-permute-done.5.refs_2_) | copy-start | bytes 5505028
  112.0 12.6 %collective-permute-start.7 = (bf16[128,1792]{1,0:T(8,128)(2,1)S(1)}, bf16[128,1792]{1,0:T(8,128)(2,1)S(1)}, u32[]{:S(2)}, u32[]{:S(2)}) collective-permute-start(bf16[128,1792]{1,0:T(8,128)(2,1)S(1)} %add_convert_fusion.2), channel_id=1, source_target_pairs={{0,3},{1,2},{2,1},{3,0},{4,7},{5,6},{6,5},{7,4},{8,11},{9,10},{10,... | collective-permute-start | bytes 1376264 | tf_op jit(solution)/shard_map/ppermute | solution.py:37
  121.2 13.3 %copy-start.15 = (bf16[128,3584]{1,0:T(8,128)(2,1)S(1)}, bf16[128,3584]{1,0:T(8,128)(2,1)}, u32[]{:S(2)}) copy-start(bf16[128,3584]{1,0:T(8,128)(2,1)} %pad_maximum_fusion) | copy-start | bytes 2752516
  121.2 13.2 %collective-permute-start.9 = (bf16[128,1792]{1,0:T(8,128)(2,1)S(1)}, bf16[128,1792]{1,0:T(8,128)(2,1)S(1)}, u32[]{:S(2)}, u32[]{:S(2)}) collective-permute-start(bf16[128,1792]{1,0:T(8,128)(2,1)S(1)} %add_convert_fusion.1), channel_id=1, source_target_pairs={{0,3},{1,2},{2,1},{3,0},{4,7},{5,6},{6,5},{7,4},{8,11},{9,10},{10,... | collective-permute-start | bytes 1376264 | tf_op jit(solution)/shard_map/ppermute | solution.py:37
  124.2 12.0 %collective-permute-start.10 = (bf16[112,1792]{1,0:T(8,128)(2,1)S(1)}, bf16[112,1792]{1,0:T(8,128)(2,1)S(1)}, u32[]{:S(2)}, u32[]{:S(2)}) collective-permute-start(bf16[112,1792]{1,0:T(8,128)(2,1)S(1)} %copy-done.19), channel_id=1, source_target_pairs={{0,1},{1,0},{2,3},{3,2},{4,5},{5,4},{6,7},{7,6},{8,9},{9,8},{10,11... | collective-permute-start | bytes 1204232 | tf_op jit(solution)/shard_map/ppermute | solution.py:33
  134.5 2.4 copy-start.30
  136.2 0.7 copy-start.20
  136.9 23.4 %collective-permute-start.11 = (bf16[128,3584]{1,0:T(8,128)(2,1)S(1)}, bf16[128,3584]{1,0:T(8,128)(2,1)}, u32[]{:S(2)}, u32[]{:S(2)}) collective-permute-start(bf16[128,3584]{1,0:T(8,128)(2,1)S(1)} %get-tuple-element.52), channel_id=1, source_target_pairs={{0,1},{1,0},{2,3},{3,2},{4,5},{5,4},{6,7},{7,6},{8,9},{9,8},{10,11... | collective-permute-start | bytes 2752520 | tf_op jit(solution)/shard_map/ppermute | solution.py:33
  137.2 35.4 %collective-permute-start.12 = (bf16[192,1792]{1,0:T(8,128)(2,1)}, bf16[192,1792]{1,0:T(8,128)(2,1)}, u32[]{:S(2)}, u32[]{:S(2)}) collective-permute-start(bf16[192,1792]{1,0:T(8,128)(2,1)} %slice.57), channel_id=1, source_target_pairs={{0,1},{1,0},{2,3},{3,2},{4,5},{5,4},{6,7},{7,6},{8,9},{9,8},{10,11... | collective-permute-start | bytes 2064392 | tf_op jit(solution)/shard_map/ppermute | solution.py:33
  141.2 32.3 %all-to-all-start.2 = ((bf16[32,8,3584]{2,1,0:T(8,128)(2,1)}), bf16[32,8,3584]{2,1,0:T(8,128)(2,1)S(1)}, u32[]{:S(2)}, u32[]{:S(2)}) async-start(bf16[32,8,3584]{2,1,0:T(8,128)(2,1)} %fusion.1), calls=%async_computation.2 | async-start | bytes 3670016 | tf_op jit(solution)/shard_map/all_to_all | solution.py:41
  173.5 1.2 copy-start.11
  174.7 47.5 %slice-start.2 = ((s8[7340032]{0:T(1024)(128)(4,1)}), s8[3145728]{0:T(1024)(128)(4,1)S(1)}, s32[]{:S(2)}) async-start(s8[7340032]{0:T(1024)(128)(4,1)} %bitcast.103), calls=%async_computation.9 | async-start | bytes 6291456
  174.7 73.5 %all-to-all-start.3 = ((bf16[32,24,3584]{2,1,0:T(8,128)(2,1)}), bf16[32,24,3584]{2,1,0:T(8,128)(2,1)}, u32[]{:S(2)}, u32[]{:S(2)}) async-start(bf16[32,24,3584]{2,1,0:T(8,128)(2,1)} %bitcast.110), calls=%async_computation.3 | async-start | bytes 11010048 | tf_op jit(solution)/shard_map/all_to_all | solution.py:41
  179.9 42.3 %collective-permute-start.13 = (bf16[256,3584]{1,0:T(8,128)(2,1)}, bf16[256,3584]{1,0:T(8,128)(2,1)S(1)}, u32[]{:S(2)}, u32[]{:S(2)}) collective-permute-start(bf16[256,3584]{1,0:T(8,128)(2,1)} %bitcast.106), channel_id=1, source_target_pairs={{0,1},{1,0},{2,3},{3,2},{4,5},{5,4},{6,7},{7,6},{8,9},{9,8},{10,11... | collective-permute-start | bytes 5505032 | tf_op jit(solution)/shard_map/ppermute | solution.py:33
  181.4 3.1 copy-start.2
  184.5 3.1 copy-start.4
  187.6 1.5 copy-start.12
  189.1 33.2 %slice-start.3 = ((s8[7340032]{0:T(1024)(128)(4,1)}), s8[4194304]{0:T(1024)(128)(4,1)S(1)}, s32[]{:S(2)}) async-start(s8[7340032]{0:T(1024)(128)(4,1)} %bitcast.103), calls=%async_computation.10 | async-start | bytes 8388608
  222.2 14.2 %slice-start = ((s8[7340032]{0:T(1024)(128)(4,1)}), s8[4194304]{0:T(1024)(128)(4,1)S(1)}, s32[]{:S(2)}) async-start(s8[7340032]{0:T(1024)(128)(4,1)} %bitcast.101), calls=%async_computation.7 | async-start | bytes 8388608
  222.2 3.2 copy-start.5
  225.5 3.7 %copy-start.21 = (bf16[112,1792]{1,0:T(8,128)(2,1)S(1)}, bf16[112,1792]{1,0:T(8,128)(2,1)}, u32[]{:S(2)}) copy-start(bf16[112,1792]{1,0:T(8,128)(2,1)} %copy-done.20) | copy-start | bytes 1204228
  225.5 11.0 %slice-start.1 = ((s8[7340032]{0:T(1024)(128)(4,1)}), s8[3145728]{0:T(1024)(128)(4,1)S(1)}, s32[]{:S(2)}) async-start(s8[7340032]{0:T(1024)(128)(4,1)} %bitcast.101), calls=%async_computation.8 | async-start | bytes 6291456
  228.8 7.7 %copy-start.9 = (bf16[512,1792]{1,0:T(8,128)(2,1)S(1)}, bf16[512,1792]{1,0:T(8,128)(2,1)}, u32[]{:S(2)}) copy-start(bf16[512,1792]{1,0:T(8,128)(2,1)} %copy-done.8) | copy-start | bytes 5505028
  228.8 7.7 %collective-permute-start.14 = (bf16[256,512]{1,0:T(8,128)(2,1)S(1)}, bf16[256,512]{1,0:T(8,128)(2,1)S(1)}, u32[]{:S(2)}, u32[]{:S(2)}) collective-permute-start(bf16[256,512]{1,0:T(8,128)(2,1)S(1)} %shard_map.119.mine_ref), channel_id=1, source_target_pairs={{0,1},{1,0},{2,3},{3,2},{4,5},{5,4},{6,7},{7,6},{8,9},{9,8},{10,11... | collective-permute-start | bytes 786440 | tf_op jit(solution)/shard_map/ppermute | solution.py:33
  241.1 1.2 copy-start.6
  242.3 1.2 copy-start.10
  248.2 43.6 %all-to-all-start.4 = ((bf16[32,16,1792]{2,1,0:T(8,128)(2,1)}), bf16[32,16,1792]{2,1,0:T(8,128)(2,1)}, u32[]{:S(2)}, u32[]{:S(2)}) async-start(bf16[32,16,1792]{2,1,0:T(8,128)(2,1)} %bitcast.105), calls=%async_computation.4 | async-start | bytes 3670016 | tf_op jit(solution)/shard_map/all_to_all | solution.py:41
  257.5 3.1 copy-start.3
  260.6 23.7 %copy-start.7 = (bf16[512,1792]{1,0:T(8,128)(2,1)S(1)}, bf16[512,1792]{1,0:T(8,128)(2,1)}, u32[]{:S(2)}) copy-start(bf16[512,1792]{1,0:T(8,128)(2,1)} %copy-done.6) | copy-start | bytes 5505028
  272.7 11.5 %collective-permute-start.15 = (bf16[384,512]{1,0:T(8,128)(2,1)S(1)}, bf16[384,512]{1,0:T(8,128)(2,1)S(1)}, u32[]{:S(2)}, u32[]{:S(2)}) collective-permute-start(bf16[384,512]{1,0:T(8,128)(2,1)S(1)} %shard_map.121.mine_ref), channel_id=1, source_target_pairs={{0,1},{1,0},{2,3},{3,2},{4,5},{5,4},{6,7},{7,6},{8,9},{9,8},{10,11... | collective-permute-start | bytes 1179656 | tf_op jit(solution)/shard_map/ppermute | solution.py:33
  291.9 7.4 %copy-start.27 = (bf16[128,8]{0,1:T(8,128)(2,1)S(1)}, bf16[128,8]{0,1:T(8,128)(2,1)}, u32[]{:S(2)}) copy-start(bf16[128,8]{0,1:T(8,128)(2,1)} %param.23) | copy-start | bytes 6148
  291.9 7.5 %copy-start.29 = (s32[32]{0:T(128)S(1)}, s32[32]{0:T(128)}, u32[]{:S(2)}) copy-start(s32[32]{0:T(128)} %copy-done.28) | copy-start | bytes 388
  291.9 43.4 %all-to-all-start.5 = ((bf16[32,24,1792]{2,1,0:T(8,128)(2,1)}), bf16[32,24,1792]{2,1,0:T(8,128)(2,1)S(1)}, u32[]{:S(2)}, u32[]{:S(2)}) async-start(bf16[32,24,1792]{2,1,0:T(8,128)(2,1)} %bitcast.34), calls=%async_computation.5 | async-start | bytes 5505024 | tf_op jit(solution)/shard_map/all_to_all | solution.py:41
  299.3 3.5 copy-start.13
  335.3 15.1 %copy-start.14 = (f32[128,1792]{1,0:T(8,128)S(1)}, f32[128,1792]{1,0:T(8,128)}, u32[]{:S(2)}) copy-start(f32[128,1792]{1,0:T(8,128)} %convolution_add_fusion.2) | copy-start | bytes 2752516
  335.3 16.4 %copy-start.1 = (bf16[128,1024]{1,0:T(8,128)(2,1)S(1)}, bf16[128,1024]{1,0:T(8,128)(2,1)}, u32[]{:S(2)}) copy-start(bf16[128,1024]{1,0:T(8,128)(2,1)} %param.12) | copy-start | bytes 786436
  337.2 13.3 %collective-permute-start.16 = (bf16[128,1792]{1,0:T(8,128)(2,1)S(1)}, bf16[128,1792]{1,0:T(8,128)(2,1)S(1)}, u32[]{:S(2)}, u32[]{:S(2)}) collective-permute-start(bf16[128,1792]{1,0:T(8,128)(2,1)S(1)} %fusion.11), channel_id=1, source_target_pairs={{0,3},{1,2},{2,1},{3,0},{4,7},{5,6},{6,5},{7,4},{8,11},{9,10},{10,... | collective-permute-start | bytes 1376264 | tf_op jit(solution)/shard_map/ppermute | solution.py:37
Sparse Core Ops, SparseCore 0:
  9.6 85.4 all-gather.1

commit v3 on v2

--- a/solution.py
+++ b/solution.py
@@ -267,7 +267,7 @@
 
     return call(
         kernel,
-        40,
+        58,
         order,
         2 * steps,
         [

time: 360 us -> 361 us (level)
    unnamed x77 -> x81, local copies, waits for them, and re-layouts: 22.6 us -> 20.5 us
where the time goes in v3:
time: 361 us; the launch traced here: 360 us
  waiting for transfers between devices  157 us (43%)
  starting transfers between devices  65.2 us (18%)
  local copies, waits for them, and re-layouts  42.8 us (12%)
  Pallas kernels  33.2 us (9%)
  matrix products  32.2 us (9%)
  other arithmetic  15.3 us (4%)
  between operations  14.1 us (4%)
    ppermute x11, waiting for transfers between devices, half_swap(): return lax.ppermute(block, 'exp', [(i, i ^ 1) for i in range(4)])  78.8 us
    all_to_all x6, waiting for transfers between devices, spread(): return lax.all_to_all(block, 'seq', split_axis=0, concat_axis=0, tiled=True)  54.4 us
    all_to_all x6, starting transfers between devices, spread(): return lax.all_to_all(block, 'seq', split_axis=0, concat_axis=0, tiled=True)  43.2 us
    pallas_call x5, Pallas kernels, call(): pl.pallas_call(kernel, grid_spec=pltpu.PrefetchScalarGridSpec(num_scalar_...  33.2 us
    ppermute x5, waiting for transfers between devices, group_swap(): return lax.ppermute(block, 'exp', [(i, 3 - i) for i in range(4)])  20.7 us
    unnamed x81, local copies, waits for them, and re-layouts  20.5 us
    dot_general x8, matrix products, dot(): return jnp.dot(a, b, preferred_element_type=F32)  17.8 us
    ppermute x5, starting transfers between devices, group_swap(): return lax.ppermute(block, 'exp', [(i, 3 - i) for i in range(4)])  12.8 us
  transfers between devices with their start and end apart: 24, of which 16 were waited for; matrix products, arithmetic and copies ran while one was open for 19% of the time, Pallas kernels for 9%

profile of v3, /device:TPU:0, one launch (start us, length us, event | category | flops | bytes accessed | tf_op | source)
XLA Modules:
  0.0 359.5 jit_solution(15136534746552736271)
XLA Ops:
  6.5 1.9 reshape.220
  9.2 4.1 %collective-permute-start.1 = (bf16[1,1792]{1,0:T(2,128)(2,1)S(1)}, bf16[1,1792]{1,0:T(2,128)(2,1)S(1)}, u32[]{:S(2)}, u32[]{:S(2)}) collective-permute-start(bf16[1,1792]{1,0:T(2,128)(2,1)S(1)} %broadcast_in_dim.131), channel_id=1, source_target_pairs={{0,3},{1,2},{2,1},{3,0},{4,7},{5,6},{6,5},{7,4},{8,11},{9,10},{10,... | collective-permute-start | bytes 10760 | tf_op jit(solution)/shard_map/ppermute | solution.py:37
  13.3 1.7 constant_dynamic-update-slice_fusion.1
  15.0 1.7 constant_dynamic-update-slice_fusion
  16.7 2.3 collective-permute-start
  18.9 8.0 %all-to-all-start = ((bf16[32,8,1024]{2,1,0:T(8,128)(2,1)}), bf16[32,8,1024]{2,1,0:T(8,128)(2,1)S(1)}, u32[]{:S(2)}, u32[]{:S(2)}) async-start(bf16[32,8,1024]{2,1,0:T(8,128)(2,1)} %bitcast.13), calls=%async_computation | async-start | bytes 1048576 | tf_op jit(solution)/shard_map/all_to_all | solution.py:41
  28.6 1.2 compare_select_fusion.5
  30.9 3.6 %dynamic-slice_bitcast_fusion = (bf16[512,1792]{1,0:T(8,128)(2,1)S(1)}, bf16[512,1792]{1,0:T(8,128)(2,1)}) fusion(bf16[1,512,7168]{2,1,0:T(8,128)(2,1)} %refs_1_.3, s32[]{:T(128)S(6)} %select_n.244, s32[]{:T(128)S(6)} %select_n.243), kind=kLoop, calls=%fused_computation.42 | loop fusion | bytes 7340040 | tf_op jit(solution)/shard_map/dynamic_slice | solution.py:369
  37.4 3.7 %collective-permute-done.2.gain_ref = bf16[1,3584]{1,0:T(2,128)(2,1)S(1)} collective-permute-done((bf16[1,3584]{1,0:T(2,128)(2,1)S(1)}, bf16[1,3584]{1,0:T(2,128)(2,1)S(1)}, u32[]{:S(2)}, u32[]{:S(2)}) %collective-permute-start.2) | collective-permute-done | bytes 7200 | tf_op jit(solution)/shard_map/ppermute | solution.py:33
  43.7 2.0 collective-permute-start.5
  45.7 1.6 gather_fusion
  47.4 2.4 bitcast_select_fusion.2
  49.7 7.4 %all-to-all-start.1 = ((bf16[32,16,1024]{2,1,0:T(8,128)(2,1)}), bf16[32,16,1024]{2,1,0:T(8,128)(2,1)S(1)}, u32[]{:S(2)}, u32[]{:S(2)}) async-start(bf16[32,16,1024]{2,1,0:T(8,128)(2,1)} %bitcast_select_fusion.2), calls=%async_computation.1 | async-start | bytes 2097152 | tf_op jit(solution)/shard_map/all_to_all | solution.py:41
  57.2 1.2 broadcast_select_fusion.1
  59.4 1.9 fusion.123
  63.3 1.8 copy.46
  65.1 19.2 %all-to-all-done.1 = bf16[32,16,1024]{2,1,0:T(8,128)(2,1)S(1)} async-done(((bf16[32,16,1024]{2,1,0:T(8,128)(2,1)}), bf16[32,16,1024]{2,1,0:T(8,128)(2,1)S(1)}, u32[]{:S(2)}, u32[]{:S(2)}) %all-to-all-start.1) | async-done | bytes 1048608 | tf_op jit(solution)/shard_map/all_to_all | solution.py:41
  85.9 3.2 fusion.126
  89.1 2.1 convolution_convert_fusion.2
  92.2 2.9 all-gather.2.cloned.1.call-done
  95.1 2.7 fusion.12
  97.8 1.6 collective-permute-start.4
  99.4 2.7 fusion.18
  102.7 2.7 fusion.15
  105.4 2.7 fusion.21
  108.1 3.6 %collective-permute-done.4 = bf16[128,1792]{1,0:T(8,128)(2,1)S(1)} collective-permute-done((bf16[128,1792]{1,0:T(8,128)(2,1)S(1)}, bf16[128,1792]{1,0:T(8,128)(2,1)S(1)}, u32[]{:S(2)}, u32[]{:S(2)}) %collective-permute-start.4) | collective-permute-done | bytes 458784 | tf_op jit(solution)/shard_map/ppermute | solution.py:33
  111.9 2.9 collective-permute-start.7
  114.8 6.2 %collective-permute-done.8 = bf16[128,1792]{1,0:T(8,128)(2,1)S(1)} collective-permute-done((bf16[128,1792]{1,0:T(8,128)(2,1)S(1)}, bf16[128,1792]{1,0:T(8,128)(2,1)S(1)}, u32[]{:S(2)}, u32[]{:S(2)}) %collective-permute-start.8) | collective-permute-done | bytes 458784 | tf_op jit(solution)/shard_map/ppermute | solution.py:33
  121.2 3.0 collective-permute-start.9
  124.8 9.7 %collective-permute-done.9 = bf16[128,1792]{1,0:T(8,128)(2,1)S(1)} collective-permute-done((bf16[128,1792]{1,0:T(8,128)(2,1)S(1)}, bf16[128,1792]{1,0:T(8,128)(2,1)S(1)}, u32[]{:S(2)}, u32[]{:S(2)}) %collective-permute-start.9) | collective-permute-done | bytes 458784 | tf_op jit(solution)/shard_map/ppermute | solution.py:37
  134.6 1.6 multiply_convert_fusion
  137.2 2.1 collective-permute-start.12
  139.3 1.9 fusion.1
  141.2 6.2 %all-to-all-start.2 = ((bf16[32,8,3584]{2,1,0:T(8,128)(2,1)}), bf16[32,8,3584]{2,1,0:T(8,128)(2,1)S(1)}, u32[]{:S(2)}, u32[]{:S(2)}) async-start(bf16[32,8,3584]{2,1,0:T(8,128)(2,1)} %fusion.1), calls=%async_computation.2 | async-start | bytes 3670016 | tf_op jit(solution)/shard_map/all_to_all | solution.py:41
  147.8 12.6 %collective-permute-done.11 = bf16[128,3584]{1,0:T(8,128)(2,1)} collective-permute-done((bf16[128,3584]{1,0:T(8,128)(2,1)S(1)}, bf16[128,3584]{1,0:T(8,128)(2,1)}, u32[]{:S(2)}, u32[]{:S(2)}) %collective-permute-start.11) | collective-permute-done | bytes 917536 | tf_op jit(solution)/shard_map/ppermute | solution.py:33
  160.3 1.5 fusion.34
  161.8 1.6 fusion.27
  163.4 4.0 %convolution_convert_fusion = bf16[768,3584]{1,0:T(8,128)(2,1)} fusion(bf16[128,3584]{1,0:T(8,128)(2,1)S(1)} %get-tuple-element.100, bf16[128,3584]{1,0:T(8,128)(2,1)S(1)} %get-tuple-element.99, pred[768,128]{1,0:T(8,128)(4,1)S(1)} %bitcast.123, pred[768,128]{1,0:T(8,128)(4,1)S(1)} %bitcast.122), kind=kOutput, calls=%fused_computation.2 | convolution fusion | flops 1415905280 | bytes 7536640 | tf_op jit(solution)/shard_map/dot_general | solution.py:25
  167.5 5.2 %collective-permute-done.12 = bf16[192,1792]{1,0:T(8,128)(2,1)} collective-permute-done((bf16[192,1792]{1,0:T(8,128)(2,1)}, bf16[192,1792]{1,0:T(8,128)(2,1)}, u32[]{:S(2)}, u32[]{:S(2)}) %collective-permute-start.12) | collective-permute-done | bytes 688160 | tf_op jit(solution)/shard_map/ppermute | solution.py:33
  174.7 5.2 %all-to-all-start.3 = ((bf16[32,24,3584]{2,1,0:T(8,128)(2,1)}), bf16[32,24,3584]{2,1,0:T(8,128)(2,1)}, u32[]{:S(2)}, u32[]{:S(2)}) async-start(bf16[32,24,3584]{2,1,0:T(8,128)(2,1)} %bitcast.110), calls=%async_computation.3 | async-start | bytes 11010048 | tf_op jit(solution)/shard_map/all_to_all | solution.py:41
  181.3 3.1 copy-done.2
  184.4 3.1 copy-done.3
  187.5 1.5 copy-done.11
  189.0 3.1 shard_map.118
  192.1 30.1 %collective-permute-done.13.x_ref = bf16[256,3584]{1,0:T(8,128)(2,1)S(1)} collective-permute-done((bf16[256,3584]{1,0:T(8,128)(2,1)}, bf16[256,3584]{1,0:T(8,128)(2,1)S(1)}, u32[]{:S(2)}, u32[]{:S(2)}) %collective-permute-start.13) | collective-permute-done | bytes 1835040 | tf_op jit(solution)/shard_map/ppermute | solution.py:33
  222.2 3.2 copy-done.4
  225.4 3.3 shard_map.119.mine_ref
  229.1 1.3 constant_dynamic-update-slice_fusion.2.refs_3_
  230.4 6.0 %collective-permute-done.14.theirs_ref = bf16[256,512]{1,0:T(8,128)(2,1)S(1)} collective-permute-done((bf16[256,512]{1,0:T(8,128)(2,1)S(1)}, bf16[256,512]{1,0:T(8,128)(2,1)S(1)}, u32[]{:S(2)}, u32[]{:S(2)}) %collective-permute-start.14) | collective-permute-done | bytes 262176 | tf_op jit(solution)/shard_map/ppermute | solution.py:33
  236.4 4.6 %shard_map.120 = bf16[512,1792]{1,0:T(8,128)(2,1)S(1)} custom-call(s32[4]{0:T(128)S(1)} %pad_add_fusion.4.order_ref, bf16[256,512]{1,0:T(8,128)(2,1)S(1)} %shard_map.119.mine_ref, bf16[256,512]{1,0:T(8,128)(2,1)S(1)} %collective-permute-done.14.theirs_ref, bf16[256,256]{1,0:T(8,128)(2,1)S(1)} %fusion.58.place_ref, bf16[1,512,7168]{2,1,0:T(8,128)(2,1)S(1)} %bitcast.102, ...), custom_call_target="tpu_custom_call" | custom-call | flops 1000 | bytes 1000 | tf_op jit(solution)/shard_map/pallas_call | solution.py:129
  242.2 1.2 copy-done.9
  243.4 4.7 %all-to-all-done.3 = bf16[32,24,3584]{2,1,0:T(8,128)(2,1)} async-done(((bf16[32,24,3584]{2,1,0:T(8,128)(2,1)}), bf16[32,24,3584]{2,1,0:T(8,128)(2,1)}, u32[]{:S(2)}, u32[]{:S(2)}) %all-to-all-start.3) | async-done | bytes 5505056 | tf_op jit(solution)/shard_map/all_to_all | solution.py:41
  248.2 9.1 %all-to-all-start.4 = ((bf16[32,16,1792]{2,1,0:T(8,128)(2,1)}), bf16[32,16,1792]{2,1,0:T(8,128)(2,1)}, u32[]{:S(2)}, u32[]{:S(2)}) async-start(bf16[32,16,1792]{2,1,0:T(8,128)(2,1)} %bitcast.105), calls=%async_computation.4 | async-start | bytes 3670016 | tf_op jit(solution)/shard_map/all_to_all | solution.py:41
  258.1 14.7 %shard_map.121.mine_ref = bf16[384,512]{1,0:T(8,128)(2,1)} custom-call(s32[4]{0:T(128)} %copy-done.13, bf16[768,3584]{1,0:T(8,128)(2,1)} %bitcast.31.x_ref, bf16[192,192]{1,0:T(8,128)(2,1)} %get-tuple-element.98.pick_ref, bf16[1,7168,512]{2,1,0:T(8,128)(2,1)} %wg_ref.5, bf16[1,7168,512]{2,1,0:T(8,128)(2,1)} %wu_ref.5), custom_call_target="tpu_custom_call" | custom-call | flops 1000 | bytes 1000 | tf_op jit(solution)/shard_map/pallas_call | solution.py:129
  272.8 11.4 %collective-permute-done.15.theirs_ref = bf16[384,512]{1,0:T(8,128)(2,1)S(1)} collective-permute-done((bf16[384,512]{1,0:T(8,128)(2,1)}, bf16[384,512]{1,0:T(8,128)(2,1)S(1)}, u32[]{:S(2)}, u32[]{:S(2)}) %collective-permute-start.15) | collective-permute-done | bytes 393248 | tf_op jit(solution)/shard_map/ppermute | solution.py:33
  285.2 7.6 %shard_map.122 = bf16[768,1792]{1,0:T(8,128)(2,1)} custom-call(s32[4]{0:T(128)S(1)} %copy-done.14, bf16[384,512]{1,0:T(8,128)(2,1)S(1)} %copy-done.12, bf16[384,512]{1,0:T(8,128)(2,1)S(1)} %collective-permute-done.15.theirs_ref, bf16[192,192]{1,0:T(8,128)(2,1)S(1)} %get-tuple-element.97.place_ref, bf16[1,512,7168]{2,1,0:T(8,128)(2,1)} %refs_1_.3, ...), custom_call_target="tpu_custom_call" | custom-call | flops 1000 | bytes 1000 | tf_op jit(solution)/shard_map/pallas_call | solution.py:129
  292.8 7.4 %all-to-all-start.5 = ((bf16[32,24,1792]{2,1,0:T(8,128)(2,1)}), bf16[32,24,1792]{2,1,0:T(8,128)(2,1)S(1)}, u32[]{:S(2)}, u32[]{:S(2)}) async-start(bf16[32,24,1792]{2,1,0:T(8,128)(2,1)} %bitcast.34), calls=%async_computation.5 | async-start | bytes 5505024 | tf_op jit(solution)/shard_map/all_to_all | solution.py:41
  300.6 3.0 fusion.131
  303.7 2.9 convolution_add_fusion.2
  306.6 29.7 %all-to-all-done.5 = bf16[32,24,1792]{2,1,0:T(8,128)(2,1)S(1)} async-done(((bf16[32,24,1792]{2,1,0:T(8,128)(2,1)}), bf16[32,24,1792]{2,1,0:T(8,128)(2,1)S(1)}, u32[]{:S(2)}, u32[]{:S(2)}) %all-to-all-start.5) | async-done | bytes 2752544 | tf_op jit(solution)/shard_map/all_to_all | solution.py:41
  336.2 1.8 fusion.11
  338.1 2.7 collective-permute-start.16
  340.8 10.6 %collective-permute-done.16 = bf16[128,1792]{1,0:T(8,128)(2,1)S(1)} collective-permute-done((bf16[128,1792]{1,0:T(8,128)(2,1)S(1)}, bf16[128,1792]{1,0:T(8,128)(2,1)S(1)}, u32[]{:S(2)}, u32[]{:S(2)}) %collective-permute-start.16) | collective-permute-done | bytes 458784 | tf_op jit(solution)/shard_map/ppermute | solution.py:37
  351.3 1.3 add_convert_fusion
  (158 shorter events, 24.5 us)
Async XLA Ops:
  6.5 79.4 %copy-start = (bf16[128,1024]{1,0:T(8,128)(2,1)S(1)}, bf16[128,1024]{1,0:T(8,128)(2,1)}, u32[]{:S(2)}) copy-start(bf16[128,1024]{1,0:T(8,128)(2,1)} %param.12) | copy-start | bytes 786436
  6.5 20.5 %copy-start.27 = (s32[32,3]{0,1:T(4,128)S(1)}, s32[32,3]{0,1:T(4,128)}, u32[]{:S(2)}) copy-start(s32[32,3]{0,1:T(4,128)} %param.15) | copy-start | bytes 1156
  6.5 23.9 %copy-start.26 = (s32[128,8]{0,1:T(8,128)S(1)}, s32[128,8]{0,1:T(8,128)}, u32[]{:S(2)}) copy-start(s32[128,8]{0,1:T(8,128)} %param.22) | copy-start | bytes 12292
  6.5 88.6 %all-gather.2.cloned.1.call-start = ((), (), s32[]{:S(2)}) async-start(), calls=%async_computation.6 | async-start | bytes 15138816 | tf_op jit(solution)/shard_map/all_gather | solution.py:362
  9.2 28.0 %collective-permute-start.1 = (bf16[1,1792]{1,0:T(2,128)(2,1)S(1)}, bf16[1,1792]{1,0:T(2,128)(2,1)S(1)}, u32[]{:S(2)}, u32[]{:S(2)}) collective-permute-start(bf16[1,1792]{1,0:T(2,128)(2,1)S(1)} %broadcast_in_dim.131), channel_id=1, source_target_pairs={{0,3},{1,2},{2,1},{3,0},{4,7},{5,6},{6,5},{7,4},{8,11},{9,10},{10,... | collective-permute-start | bytes 10760 | tf_op jit(solution)/shard_map/ppermute | solution.py:37
  16.7 42.8 %collective-permute-start = (bf16[256,1024]{1,0:T(8,128)(2,1)}, bf16[256,1024]{1,0:T(8,128)(2,1)}, u32[]{:S(2)}, u32[]{:S(2)}) collective-permute-start(bf16[256,1024]{1,0:T(8,128)(2,1)} %constant_dynamic-update-slice_fusion), channel_id=1, source_target_pairs={{0,4},{4,8},{8,12},{12,16},{16,20},{20,24},{24,28},{28,32},{32,36}... | collective-permute-start | bytes 1572872 | tf_op jit(solution)/shard_map/ppermute | solution.py:50
  18.9 26.8 %all-to-all-start = ((bf16[32,8,1024]{2,1,0:T(8,128)(2,1)}), bf16[32,8,1024]{2,1,0:T(8,128)(2,1)S(1)}, u32[]{:S(2)}, u32[]{:S(2)}) async-start(bf16[32,8,1024]{2,1,0:T(8,128)(2,1)} %bitcast.13), calls=%async_computation | async-start | bytes 1048576 | tf_op jit(solution)/shard_map/all_to_all | solution.py:41
  26.9 30.2 %collective-permute-start.3 = (bf16[128,1792]{1,0:T(8,128)(2,1)}, bf16[128,1792]{1,0:T(8,128)(2,1)}, u32[]{:S(2)}, u32[]{:S(2)}) collective-permute-start(bf16[128,1792]{1,0:T(8,128)(2,1)} %param.16), channel_id=1, source_target_pairs={{0,3},{1,2},{2,1},{3,0},{4,7},{5,6},{6,5},{7,4},{8,11},{9,10},{10,... | collective-permute-start | bytes 1376264 | tf_op jit(solution)/shard_map/ppermute | solution.py:37
  28.0 2.6 copy-start.30
  30.9 4.2 %copy-start.18 = (bf16[128,1024]{1,0:T(8,128)(2,1)S(1)}, bf16[128,1024]{1,0:T(8,128)(2,1)}, u32[]{:S(2)}) copy-start(bf16[128,1024]{1,0:T(8,128)(2,1)} %param.13) | copy-start | bytes 786436
  30.9 4.4 %copy-start.19 = (bf16[128,1024]{1,0:T(8,128)(2,1)S(1)}, bf16[128,1024]{1,0:T(8,128)(2,1)}, u32[]{:S(2)}) copy-start(bf16[128,1024]{1,0:T(8,128)(2,1)} %param.14) | copy-start | bytes 786436
  30.9 6.3 %copy-start.25 = (bf16[1792]{0:T(1024)(128)(2,1)S(1)}, bf16[1792]{0:T(1024)(128)(2,1)}, u32[]{:S(2)}) copy-start(bf16[1792]{0:T(1024)(128)(2,1)} %param.18) | copy-start | bytes 10756
  37.3 3.8 %collective-permute-start.2 = (bf16[1,3584]{1,0:T(2,128)(2,1)S(1)}, bf16[1,3584]{1,0:T(2,128)(2,1)S(1)}, u32[]{:S(2)}, u32[]{:S(2)}) collective-permute-start(bf16[1,3584]{1,0:T(2,128)(2,1)S(1)} %pad_maximum_fusion.1.gain_ref), channel_id=1, source_target_pairs={{0,1},{1,0},{2,3},{3,2},{4,5},{5,4},{6,7},{7,6},{8,9},{9,8},{10,11... | collective-permute-start | bytes 21512 | tf_op jit(solution)/shard_map/ppermute | solution.py:33
  43.7 68.0 %collective-permute-start.6 = (bf16[208,1792]{1,0:T(8,128)(2,1)}, bf16[208,1792]{1,0:T(8,128)(2,1)}, u32[]{:S(2)}, u32[]{:S(2)}) collective-permute-start(bf16[208,1792]{1,0:T(8,128)(2,1)} %slice.58), channel_id=1, source_target_pairs={{0,1},{1,0},{2,3},{3,2},{4,5},{5,4},{6,7},{7,6},{8,9},{9,8},{10,11... | collective-permute-start | bytes 2236424 | tf_op jit(solution)/shard_map/ppermute | solution.py:33
  43.7 68.0 %collective-permute-start.5 = (bf16[512,1792]{1,0:T(8,128)(2,1)}, bf16[512,1792]{1,0:T(8,128)(2,1)S(1)}, u32[]{:S(2)}, u32[]{:S(2)}) collective-permute-start(bf16[512,1792]{1,0:T(8,128)(2,1)} %get-tuple-element.46), channel_id=1, source_target_pairs={{0,1},{1,0},{2,3},{3,2},{4,5},{5,4},{6,7},{7,6},{8,9},{9,8},{10,11... | collective-permute-start | bytes 5505032 | tf_op jit(solution)/shard_map/ppermute | solution.py:33
  49.7 34.6 %all-to-all-start.1 = ((bf16[32,16,1024]{2,1,0:T(8,128)(2,1)}), bf16[32,16,1024]{2,1,0:T(8,128)(2,1)S(1)}, u32[]{:S(2)}, u32[]{:S(2)}) async-start(bf16[32,16,1024]{2,1,0:T(8,128)(2,1)} %bitcast_select_fusion.2), calls=%async_computation.1 | async-start | bytes 2097152 | tf_op jit(solution)/shard_map/all_to_all | solution.py:41
  85.9 3.2 copy-start.20
  85.9 3.2 copy-start.24
  89.1 2.1 copy-start.28
  97.8 13.9 %collective-permute-start.4 = (bf16[128,1792]{1,0:T(8,128)(2,1)S(1)}, bf16[128,1792]{1,0:T(8,128)(2,1)S(1)}, u32[]{:S(2)}, u32[]{:S(2)}) collective-permute-start(bf16[128,1792]{1,0:T(8,128)(2,1)S(1)} %fusion.12), channel_id=1, source_target_pairs={{0,1},{1,0},{2,3},{3,2},{4,5},{5,4},{6,7},{7,6},{8,9},{9,8},{10,11... | collective-permute-start | bytes 1376264 | tf_op jit(solution)/shard_map/ppermute | solution.py:33
  102.1 18.9 %collective-permute-start.8 = (bf16[128,1792]{1,0:T(8,128)(2,1)S(1)}, bf16[128,1792]{1,0:T(8,128)(2,1)S(1)}, u32[]{:S(2)}, u32[]{:S(2)}) collective-permute-start(bf16[128,1792]{1,0:T(8,128)(2,1)S(1)} %fusion.18), channel_id=1, source_target_pairs={{0,1},{1,0},{2,3},{3,2},{4,5},{5,4},{6,7},{7,6},{8,9},{9,8},{10,11... | collective-permute-start | bytes 1376264 | tf_op jit(solution)/shard_map/ppermute | solution.py:33
  108.1 16.1 %copy-start.21 = (bf16[112,1792]{1,0:T(8,128)(2,1)S(1)}, bf16[112,1792]{1,0:T(8,128)(2,1)}, u32[]{:S(2)}) copy-start(bf16[112,1792]{1,0:T(8,128)(2,1)} %slice.56) | copy-start | bytes 1204228
  111.7 13.0 %copy-start.7 = (bf16[512,1792]{1,0:T(8,128)(2,1)}, bf16[512,1792]{1,0:T(8,128)(2,1)S(1)}, u32[]{:S(2)}) copy-start(bf16[512,1792]{1,0:T(8,128)(2,1)S(1)} %collective-permute-done.5.refs_2_) | copy-start | bytes 5505028
  111.9 12.7 %collective-permute-start.7 = (bf16[128,1792]{1,0:T(8,128)(2,1)S(1)}, bf16[128,1792]{1,0:T(8,128)(2,1)S(1)}, u32[]{:S(2)}, u32[]{:S(2)}) collective-permute-start(bf16[128,1792]{1,0:T(8,128)(2,1)S(1)} %add_convert_fusion.2), channel_id=1, source_target_pairs={{0,3},{1,2},{2,1},{3,0},{4,7},{5,6},{6,5},{7,4},{8,11},{9,10},{10,... | collective-permute-start | bytes 1376264 | tf_op jit(solution)/shard_map/ppermute | solution.py:37
  121.2 13.4 %copy-start.17 = (bf16[128,3584]{1,0:T(8,128)(2,1)S(1)}, bf16[128,3584]{1,0:T(8,128)(2,1)}, u32[]{:S(2)}) copy-start(bf16[128,3584]{1,0:T(8,128)(2,1)} %pad_maximum_fusion) | copy-start | bytes 2752516
  121.2 13.3 %collective-permute-start.9 = (bf16[128,1792]{1,0:T(8,128)(2,1)S(1)}, bf16[128,1792]{1,0:T(8,128)(2,1)S(1)}, u32[]{:S(2)}, u32[]{:S(2)}) collective-permute-start(bf16[128,1792]{1,0:T(8,128)(2,1)S(1)} %add_convert_fusion.1), channel_id=1, source_target_pairs={{0,3},{1,2},{2,1},{3,0},{4,7},{5,6},{6,5},{7,4},{8,11},{9,10},{10,... | collective-permute-start | bytes 1376264 | tf_op jit(solution)/shard_map/ppermute | solution.py:37
  124.1 12.0 %collective-permute-start.10 = (bf16[112,1792]{1,0:T(8,128)(2,1)S(1)}, bf16[112,1792]{1,0:T(8,128)(2,1)S(1)}, u32[]{:S(2)}, u32[]{:S(2)}) collective-permute-start(bf16[112,1792]{1,0:T(8,128)(2,1)S(1)} %copy-done.21), channel_id=1, source_target_pairs={{0,1},{1,0},{2,3},{3,2},{4,5},{5,4},{6,7},{7,6},{8,9},{9,8},{10,11... | collective-permute-start | bytes 1204232 | tf_op jit(solution)/shard_map/ppermute | solution.py:33
  134.6 2.4 copy-start.32
  136.2 0.7 copy-start.22
  136.9 23.4 %collective-permute-start.11 = (bf16[128,3584]{1,0:T(8,128)(2,1)S(1)}, bf16[128,3584]{1,0:T(8,128)(2,1)}, u32[]{:S(2)}, u32[]{:S(2)}) collective-permute-start(bf16[128,3584]{1,0:T(8,128)(2,1)S(1)} %get-tuple-element.52), channel_id=1, source_target_pairs={{0,1},{1,0},{2,3},{3,2},{4,5},{5,4},{6,7},{7,6},{8,9},{9,8},{10,11... | collective-permute-start | bytes 2752520 | tf_op jit(solution)/shard_map/ppermute | solution.py:33
  137.2 35.5 %collective-permute-start.12 = (bf16[192,1792]{1,0:T(8,128)(2,1)}, bf16[192,1792]{1,0:T(8,128)(2,1)}, u32[]{:S(2)}, u32[]{:S(2)}) collective-permute-start(bf16[192,1792]{1,0:T(8,128)(2,1)} %slice.57), channel_id=1, source_target_pairs={{0,1},{1,0},{2,3},{3,2},{4,5},{5,4},{6,7},{7,6},{8,9},{9,8},{10,11... | collective-permute-start | bytes 2064392 | tf_op jit(solution)/shard_map/ppermute | solution.py:33
  141.2 32.2 %all-to-all-start.2 = ((bf16[32,8,3584]{2,1,0:T(8,128)(2,1)}), bf16[32,8,3584]{2,1,0:T(8,128)(2,1)S(1)}, u32[]{:S(2)}, u32[]{:S(2)}) async-start(bf16[32,8,3584]{2,1,0:T(8,128)(2,1)} %fusion.1), calls=%async_computation.2 | async-start | bytes 3670016 | tf_op jit(solution)/shard_map/all_to_all | solution.py:41
  173.4 1.2 copy-start.10
  174.7 47.5 %slice-start.2 = ((s8[7340032]{0:T(1024)(128)(4,1)}), s8[3145728]{0:T(1024)(128)(4,1)S(1)}, s32[]{:S(2)}) async-start(s8[7340032]{0:T(1024)(128)(4,1)} %bitcast.103), calls=%async_computation.9 | async-start | bytes 6291456
  174.7 73.5 %all-to-all-start.3 = ((bf16[32,24,3584]{2,1,0:T(8,128)(2,1)}), bf16[32,24,3584]{2,1,0:T(8,128)(2,1)}, u32[]{:S(2)}, u32[]{:S(2)}) async-start(bf16[32,24,3584]{2,1,0:T(8,128)(2,1)} %bitcast.110), calls=%async_computation.3 | async-start | bytes 11010048 | tf_op jit(solution)/shard_map/all_to_all | solution.py:41
  179.8 42.3 %collective-permute-start.13 = (bf16[256,3584]{1,0:T(8,128)(2,1)}, bf16[256,3584]{1,0:T(8,128)(2,1)S(1)}, u32[]{:S(2)}, u32[]{:S(2)}) collective-permute-start(bf16[256,3584]{1,0:T(8,128)(2,1)} %bitcast.106), channel_id=1, source_target_pairs={{0,1},{1,0},{2,3},{3,2},{4,5},{5,4},{6,7},{7,6},{8,9},{9,8},{10,11... | collective-permute-start | bytes 5505032 | tf_op jit(solution)/shard_map/ppermute | solution.py:33
  180.0 56.4 %copy-start.13 = (s32[4]{0:T(128)}, s32[4]{0:T(128)S(1)}, u32[]{:S(2)}) copy-start(s32[4]{0:T(128)S(1)} %pad_add_fusion.4.order_ref) | copy-start | bytes 52
  181.3 3.1 copy-start.2
  184.4 3.1 copy-start.3
  187.5 1.5 copy-start.11
  189.0 33.2 %slice-start.3 = ((s8[7340032]{0:T(1024)(128)(4,1)}), s8[4194304]{0:T(1024)(128)(4,1)S(1)}, s32[]{:S(2)}) async-start(s8[7340032]{0:T(1024)(128)(4,1)} %bitcast.103), calls=%async_computation.10 | async-start | bytes 8388608
  222.1 14.2 %slice-start = ((s8[7340032]{0:T(1024)(128)(4,1)}), s8[4194304]{0:T(1024)(128)(4,1)S(1)}, s32[]{:S(2)}) async-start(s8[7340032]{0:T(1024)(128)(4,1)} %bitcast.101), calls=%async_computation.7 | async-start | bytes 8388608
  222.2 3.2 copy-start.4
  225.4 3.7 %copy-start.23 = (bf16[112,1792]{1,0:T(8,128)(2,1)S(1)}, bf16[112,1792]{1,0:T(8,128)(2,1)}, u32[]{:S(2)}) copy-start(bf16[112,1792]{1,0:T(8,128)(2,1)} %copy-done.22) | copy-start | bytes 1204228
  225.4 11.0 %slice-start.1 = ((s8[7340032]{0:T(1024)(128)(4,1)}), s8[3145728]{0:T(1024)(128)(4,1)S(1)}, s32[]{:S(2)}) async-start(s8[7340032]{0:T(1024)(128)(4,1)} %bitcast.101), calls=%async_computation.8 | async-start | bytes 6291456
  228.7 7.7 %copy-start.8 = (bf16[512,1792]{1,0:T(8,128)(2,1)S(1)}, bf16[512,1792]{1,0:T(8,128)(2,1)}, u32[]{:S(2)}) copy-start(bf16[512,1792]{1,0:T(8,128)(2,1)} %copy-done.7) | copy-start | bytes 5505028
  228.7 7.7 %collective-permute-start.14 = (bf16[256,512]{1,0:T(8,128)(2,1)S(1)}, bf16[256,512]{1,0:T(8,128)(2,1)S(1)}, u32[]{:S(2)}, u32[]{:S(2)}) collective-permute-start(bf16[256,512]{1,0:T(8,128)(2,1)S(1)} %shard_map.119.mine_ref), channel_id=1, source_target_pairs={{0,1},{1,0},{2,3},{3,2},{4,5},{5,4},{6,7},{7,6},{8,9},{9,8},{10,11... | collective-permute-start | bytes 786440 | tf_op jit(solution)/shard_map/ppermute | solution.py:33
  241.0 1.2 copy-start.5
  242.2 1.2 copy-start.9
  248.2 44.6 %all-to-all-start.4 = ((bf16[32,16,1792]{2,1,0:T(8,128)(2,1)}), bf16[32,16,1792]{2,1,0:T(8,128)(2,1)}, u32[]{:S(2)}, u32[]{:S(2)}) async-start(bf16[32,16,1792]{2,1,0:T(8,128)(2,1)} %bitcast.105), calls=%async_computation.4 | async-start | bytes 3670016 | tf_op jit(solution)/shard_map/all_to_all | solution.py:41
  258.1 26.1 %copy-start.6 = (bf16[512,1792]{1,0:T(8,128)(2,1)S(1)}, bf16[512,1792]{1,0:T(8,128)(2,1)}, u32[]{:S(2)}) copy-start(bf16[512,1792]{1,0:T(8,128)(2,1)} %copy-done.5) | copy-start | bytes 5505028
  258.1 26.1 %copy-start.14 = (s32[4]{0:T(128)S(1)}, s32[4]{0:T(128)}, u32[]{:S(2)}) copy-start(s32[4]{0:T(128)} %copy-done.13) | copy-start | bytes 52
  272.7 11.4 %collective-permute-start.15 = (bf16[384,512]{1,0:T(8,128)(2,1)}, bf16[384,512]{1,0:T(8,128)(2,1)S(1)}, u32[]{:S(2)}, u32[]{:S(2)}) collective-permute-start(bf16[384,512]{1,0:T(8,128)(2,1)} %shard_map.121.mine_ref), channel_id=1, source_target_pairs={{0,1},{1,0},{2,3},{3,2},{4,5},{5,4},{6,7},{7,6},{8,9},{9,8},{10,11... | collective-permute-start | bytes 1179656 | tf_op jit(solution)/shard_map/ppermute | solution.py:33
  284.2 1.0 copy-start.12
  292.8 7.4 %copy-start.29 = (bf16[128,8]{0,1:T(8,128)(2,1)S(1)}, bf16[128,8]{0,1:T(8,128)(2,1)}, u32[]{:S(2)}) copy-start(bf16[128,8]{0,1:T(8,128)(2,1)} %param.23) | copy-start | bytes 6148
  292.8 7.5 %copy-start.31 = (s32[32]{0:T(128)S(1)}, s32[32]{0:T(128)}, u32[]{:S(2)}) copy-start(s32[32]{0:T(128)} %copy-done.30) | copy-start | bytes 388
  292.8 43.4 %all-to-all-start.5 = ((bf16[32,24,1792]{2,1,0:T(8,128)(2,1)}), bf16[32,24,1792]{2,1,0:T(8,128)(2,1)S(1)}, u32[]{:S(2)}, u32[]{:S(2)}) async-start(bf16[32,24,1792]{2,1,0:T(8,128)(2,1)} %bitcast.34), calls=%async_computation.5 | async-start | bytes 5505024 | tf_op jit(solution)/shard_map/all_to_all | solution.py:41
  300.2 3.5 copy-start.15
  336.2 15.1 %copy-start.16 = (f32[128,1792]{1,0:T(8,128)S(1)}, f32[128,1792]{1,0:T(8,128)}, u32[]{:S(2)}) copy-start(f32[128,1792]{1,0:T(8,128)} %convolution_add_fusion.2) | copy-start | bytes 2752516
  336.2 16.4 %copy-start.1 = (bf16[128,1024]{1,0:T(8,128)(2,1)S(1)}, bf16[128,1024]{1,0:T(8,128)(2,1)}, u32[]{:S(2)}) copy-start(bf16[128,1024]{1,0:T(8,128)(2,1)} %param.12) | copy-start | bytes 786436
  338.1 13.3 %collective-permute-start.16 = (bf16[128,1792]{1,0:T(8,128)(2,1)S(1)}, bf16[128,1792]{1,0:T(8,128)(2,1)S(1)}, u32[]{:S(2)}, u32[]{:S(2)}) collective-permute-start(bf16[128,1792]{1,0:T(8,128)(2,1)S(1)} %fusion.11), channel_id=1, source_target_pairs={{0,3},{1,2},{2,1},{3,0},{4,7},{5,6},{6,5},{7,4},{8,11},{9,10},{10,... | collective-permute-start | bytes 1376264 | tf_op jit(solution)/shard_map/ppermute | solution.py:37
Sparse Core Ops, SparseCore 0:
  9.6 85.4 all-gather.1
